TPU v7x, 128 devices: a whole 4x4x4 slice. The times are simulated.
128 devices in a mesh: inner: 8 (over x, core), outer: 16 (over z, y).
Axes of the slice: x: 4, y: 4, z: 4, core: 2. Of those that a mesh axis runs over, the one named last changes fastest.
Arguments:
- features: bfloat16 [4096, 16, 512], P(('inner', 'outer')), may hold values from -24 to 24
- cotangent: bfloat16 [4096, 16, 512], P(('inner', 'outer')), may hold values from -6 to 6
- counts: int32 [128], P(('inner', 'outer')), may hold values from 5 to 32, as said below
- senders: int32 [4, 4096], P(None, ('inner', 'outer')), may hold values from 0 to 31, as said below
- angular: float32 [16, 4, 4096], P(None, None, ('inner', 'outer')), may hold values from -5 to 5
- basis: float32 [8, 4, 4096], P(None, None, ('inner', 'outer')), may hold values from -1 to 1
- species: int32 [4096], P(('inner', 'outer')), may hold values from 0 to 88
- w_up: bfloat16 [2, 4, 512, 512], replicated, may hold values from -0.25 to 0.25
- w_first: float32 [2, 8, 64], replicated, may hold values from -2 to 2
- w_second: bfloat16 [2, 64, 2048], replicated, may hold values from -0.75 to 0.75
- w_out: bfloat16 [2, 4, 512, 512], replicated, may hold values from -0.25 to 0.25
- gain: float32 [2, 89, 512], replicated, may hold values from 0.25 to 1.75
Outputs:
- up_grad: float32 [2, 4, 512, 512], P(None, None, ('inner', 'outer'))
- first_grad: float32 [2, 8, 64], replicated
- second_grad: float32 [2, 64, 2048], P(None, None, ('inner', 'outer'))
- out_grad: float32 [2, 4, 512, 512], P(None, None, ('inner', 'outer'))
- gain_grad: float32 [2, 89, 512], P(None, None, ('inner', 'outer'))
- feature_grad: bfloat16 [4096, 16, 512], P(('inner', 'outer'))
Inputs may be any that keep to these rules, and one draw needn't show every extreme that they name: `counts`: one device holds exactly 32 live atoms; the others hold between 5 and 16. `senders`: every entry is below the count of the device that holds it.
All inputs are finite; a program needn't handle non-finite values.
Results may differ from a plain program's by a relative error of at most 0.023.
Values sent between devices are 32-bit elements; how exact they have to be, the bound alone decides.
A program may use at most 128 MiB of HBM per device.

v0:
```python
import jax
import jax.numpy as jnp
from jax import lax
from jax.sharding import PartitionSpec as P

LEVELS = ((0, 1, 0), (1, 4, 1), (4, 9, 2), (9, 16, 3))
CLIP_NORM = 2048.0


def mix(values, weight):
    rows = values.shape[0]
    width = values.shape[2]
    pieces = []
    for first, last, order in LEVELS:
        block = values[:, first:last, :].reshape(rows * (last - first), width)
        pieces.append(
            jnp.dot(block, weight[order], preferred_element_type=jnp.float32).reshape(
                rows, last - first, weight.shape[2]
            )
        )
    return jnp.concatenate(pieces, axis=1)


def expand(radial):
    return jnp.concatenate(
        [
            jnp.repeat(radial[:, order : order + 1, :], last - first, axis=1)
            for first, last, order in LEVELS
        ],
        axis=1,
    )


def interaction(feats, w_up, w_first, w_second, w_out, gain, senders, angular, basis, onehot):
    rows = feats.shape[0]
    width = feats.shape[2]
    slots = senders.shape[0]
    lifted = mix(feats, w_up).astype(jnp.bfloat16)
    flat_basis = jnp.transpose(basis, (1, 2, 0)).reshape(slots * rows, basis.shape[0])
    hidden = jax.nn.silu(jnp.dot(flat_basis, w_first, precision=lax.Precision.HIGHEST)).astype(
        jnp.bfloat16
    )
    radial = jnp.dot(hidden, w_second, preferred_element_type=jnp.float32).reshape(
        slots, rows, 4, width
    )
    angular_t = jnp.transpose(angular, (1, 2, 0))

    def slot_step(total, inputs):
        index, weights, harmonics = inputs
        source = jnp.take(lifted, index, axis=0).astype(jnp.float32)
        message = expand(weights) * (harmonics[:, :, None] * source[:, 0:1, :] + source)
        return (total + message, None)

    total, unused = lax.scan(
        jax.checkpoint(slot_step),
        jnp.zeros((rows, feats.shape[1], width), jnp.float32),
        (senders, radial, angular_t),
    )
    summed = (total / slots).astype(jnp.bfloat16)
    mixed = mix(summed, w_out)
    scalar = mixed[:, 0, :]
    gates = jax.nn.sigmoid(scalar)
    skip_gain = jnp.dot(onehot, gain, precision=lax.Precision.HIGHEST)
    result = jnp.concatenate(
        [jax.nn.silu(scalar)[:, None, :], mixed[:, 1:, :] * gates[:, None, :]], axis=1
    )
    return result + skip_gain[:, None, :] * feats.astype(jnp.float32)


def device_grads(params, feats, cot, count, senders, angular, basis, species):
    rows = feats.shape[0]
    onehot = (species[:, None] == jnp.arange(params[4].shape[1], dtype=jnp.int32)[None, :]).astype(
        jnp.float32
    )
    live = (jnp.arange(rows, dtype=jnp.int32) < count).astype(jnp.float32)

    def loss_of(weights, inputs):
        w_up, w_first, w_second, w_out, gain = weights
        first = interaction(
            inputs,
            w_up[0],
            w_first[0],
            w_second[0],
            w_out[0],
            gain[0],
            senders,
            angular,
            basis,
            onehot,
        ).astype(jnp.bfloat16)
        second = interaction(
            first,
            w_up[1],
            w_first[1],
            w_second[1],
            w_out[1],
            gain[1],
            senders,
            angular,
            basis,
            onehot,
        )
        return jnp.sum(second * cot.astype(jnp.float32) * live[:, None, None])

    loss, pullback = jax.vjp(loss_of, params, feats)
    weight_grads, feat_grad = pullback(jnp.ones((), jnp.float32))
    return (tuple((g.astype(jnp.float32) for g in weight_grads)), feat_grad)


def per_device(
    features,
    cotangent,
    counts,
    senders,
    angular,
    basis,
    species,
    w_up,
    w_first,
    w_second,
    w_out,
    gain,
):
    params = (w_up, w_first, w_second, w_out, gain)
    grads, feature_grad = device_grads(
        params, features, cotangent, counts[0], senders, angular, basis, species
    )
    up_term, first_term, second_term, out_term, gain_term = grads
    shares = (
        lax.psum_scatter(up_term, ("inner", "outer"), scatter_dimension=2, tiled=True),
        lax.psum_scatter(second_term, ("inner", "outer"), scatter_dimension=2, tiled=True),
        lax.psum_scatter(out_term, ("inner", "outer"), scatter_dimension=2, tiled=True),
        lax.psum_scatter(gain_term, ("inner", "outer"), scatter_dimension=2, tiled=True),
    )
    local_squares = sum((jnp.sum(s * s) for s in shares))
    first_sum, squares = lax.psum((first_term, local_squares), ("inner", "outer"))
    squares = squares + jnp.sum(first_sum * first_sum)
    scale = jnp.minimum(1.0, CLIP_NORM / jnp.sqrt(squares + 1e-06))
    up_share, second_share, out_share, gain_share = shares
    return (
        up_share * scale,
        first_sum * scale,
        second_share * scale,
        out_share * scale,
        gain_share * scale,
        feature_grad,
    )


def solution(mesh):
    return jax.shard_map(
        per_device,
        mesh=mesh,
        in_specs=(
            P(("inner", "outer"), None, None),
            P(("inner", "outer"), None, None),
            P(("inner", "outer")),
            P(None, ("inner", "outer")),
            P(None, None, ("inner", "outer")),
            P(None, None, ("inner", "outer")),
            P(("inner", "outer")),
            P(),
            P(),
            P(),
            P(),
            P(),
        ),
        out_specs=(
            P(None, None, ("inner", "outer"), None),
            P(),
            P(None, None, ("inner", "outer")),
            P(None, None, ("inner", "outer"), None),
            P(None, None, ("inner", "outer")),
            P(("inner", "outer"), None, None),
        ),
        check_vma=False,
    )
```

profile of v0, /device:TPU:1, one launch (start us, length us, event | category | flops | bytes accessed | tf_op | source)
XLA Modules:
  0.0 606.8 jit_solution(3689812981838153123)
XLA Ops:
  11.1 2.1 convolution_convert_fusion.19
  26.5 31.4 %while.60 = (s32[]{:T(128)}, f32[32,16,512]{2,1,0:T(8,128)S(1)}, f32[4,32,4,512]{3,2,1,0:T(4,128)}, f32[4,32,16]{2,1,0:T(8,128)}, s32[4,32]{1,0:T(4,128)}, /*ind...) while((s32[]{:T(128)}, f32[32,16,512]{2,1,0:T(8,128)S(1)}, f32[4,32,4,512]{3,2,1,0:T(4,128)}, ...), condition=%wide.region_1.3_spmd.clone, body=%wide.region_0.2_spmd.clone.sunk | while | flops 3146947 | bytes 9251539 | solution.py:54
  72.0 31.6 %while.61 = (s32[]{:T(128)}, f32[32,16,512]{2,1,0:T(8,128)S(1)}, f32[4,32,4,512]{3,2,1,0:T(4,128)}, f32[4,32,16]{2,1,0:T(8,128)}, s32[4,32]{1,0:T(4,128)}, /*ind...) while((s32[]{:T(128)}, f32[32,16,512]{2,1,0:T(8,128)S(1)}, f32[4,32,4,512]{3,2,1,0:T(4,128)}, ...), condition=%wide.region_3.5_spmd.clone, body=%wide.region_2.4_spmd.clone.sunk | while | flops 3146947 | bytes 9251539 | solution.py:54
  123.3 50.7 %while.58 = (s32[]{:T(128)}, bf16[32,16,512]{2,1,0:T(8,128)(2,1)}, f32[32,16,512]{2,1,0:T(8,128)S(1)}, bf16[4,32,4,512]{3,2,1,0:T(4,128)(2,1)}, s32[4,32]{1,0:T(...) while((s32[]{:T(128)}, bf16[32,16,512]{2,1,0:T(8,128)(2,1)}, ...), condition=%wide.region_11.14_spmd, body=%wide.region_5.13_spmd.sunk | while | flops 5686563 | bytes 16002285 | solution.py:54
  129.4 5.1 scatter_fusion
  142.1 5.0 scatter_fusion
  154.7 5.0 scatter_fusion
  167.3 5.1 scatter_fusion
  199.0 60.4 %while.59 = (s32[]{:T(128)}, bf16[32,16,512]{2,1,0:T(8,128)(2,1)}, f32[32,16,512]{2,1,0:T(8,128)S(1)}, bf16[4,32,4,512]{3,2,1,0:T(4,128)(2,1)}, s32[4,32]{1,0:T(...) while((s32[]{:T(128)}, bf16[32,16,512]{2,1,0:T(8,128)(2,1)}, ...), condition=%wide.region_19.22_spmd, body=%wide.region_13.21_spmd.sunk | while | flops 5686563 | bytes 16002869 | solution.py:54
  207.4 5.2 scatter_fusion.1
  222.4 5.2 scatter_fusion.1
  237.5 5.2 scatter_fusion.1
  252.5 5.2 scatter_fusion.1
  260.8 2.5 fusion.36
  263.3 2.2 fusion.38
  267.0 2.2 fusion.33
  277.1 2.3 copy.170
  279.4 2.2 add_bitcast_fusion.2
  281.6 4.1 add_convert_fusion.3
  286.2 3.8 add_convert_fusion.2
  295.8 2.0 convolution_convert_fusion.14
  302.4 2.2 convolution_convert_fusion.8
  312.3 205.1 %all-reduce.62.cloned.1.call-done = (f32[2,4,512,512]{3,2,1,0:T(8,128)}, f32[2,64,2048]{1,0,2:T(2,128)}, f32[2,4,512,512]{3,2,1,0:T(8,128)}, f32[2,89,512]{1,0,2:T(2,128)}) async-done(((f32[2,4,512,512]{3,2,1,0:T(8,128)}, f32[2,64,2048]{1,0,2:T(2,128)}, f32[2,4,512,512]{3,2,1,0:T(8,128)}, f32[2,89,512]{1,0,2:T(2,128)}), (f32[2,4,512,512]{3,2,1,0:T(8,128)}, f32[2,64,2048]{1,0,2:T(2,128)}, ...) | async-done | bytes 18190352
  526.7 64.5 %all-reduce.58 = (f32[]{:T(128)}, f32[2,8,64]{2,1,0:T(8,128)S(1)}) all-reduce(f32[]{:T(128)S(6)} %add.247, f32[2,8,64]{2,1,0:T(8,128)S(1)} %pad_add_fusion.3), channel_id=1, replica_groups=mesh['inner'=8,'outer'=16] {'inner','outer'}, use_global_device_ids=true, to_apply=%region_30.33 | all-reduce | flops 1025 | bytes 8200 | tf_op jit(solution)/shard_map/psum | solution.py:136
  (630 shorter events, 247.5 us)
Async XLA Ops:
  7.2 15.9 %copy-start.15 = (bf16[2,64,2048]{2,1,0:T(8,128)(2,1)S(1)}, bf16[2,64,2048]{2,1,0:T(8,128)(2,1)}, u32[]{:S(2)}) copy-start(bf16[2,64,2048]{2,1,0:T(8,128)(2,1)} %param.33) | copy-start | bytes 1572868
  7.2 510.2 %all-reduce.62.cloned.1.call-start = ((), (), s32[]{:S(2)}) async-start(), calls=%async_computation | async-start | bytes 38797312
  11.1 13.7 %copy-start.42 = (bf16[128,64]{0,1:T(8,128)(2,1)}, bf16[128,64]{0,1:T(8,128)(2,1)S(1)}, u32[]{:S(2)}) copy-start(bf16[128,64]{0,1:T(8,128)(2,1)S(1)} %get-tuple-element.676) | copy-start | bytes 49156
  17.5 9.0 %copy-start.10 = (bf16[32,16,512]{2,0,1:T(8,128)(2,1)}, bf16[32,16,512]{2,0,1:T(8,128)(2,1)S(1)}, u32[]{:S(2)}) copy-start(bf16[32,16,512]{2,0,1:T(8,128)(2,1)S(1)} %copy.118) | copy-start | bytes 1572868
  57.9 7.0 %copy-start.40 = (f32[2,89,512]{2,0,1:T(2,128)S(1)}, f32[2,89,512]{2,0,1:T(2,128)}, u32[]{:S(2)}) copy-start(f32[2,89,512]{2,0,1:T(2,128)} %param.35) | copy-start | bytes 1093636
  57.9 8.0 %copy-start.49 = (s32[32]{0:T(128)S(1)}, s32[32]{0:T(128)}, u32[]{:S(2)}) copy-start(s32[32]{0:T(128)} %param.30) | copy-start | bytes 388
  57.9 8.6 %copy-start.2 = (bf16[32,16,512]{2,1,0:T(8,128)(2,1)S(1)}, bf16[32,16,512]{2,1,0:T(8,128)(2,1)}, u32[]{:S(2)}) copy-start(bf16[32,16,512]{2,1,0:T(8,128)(2,1)} %param.24) | copy-start | bytes 1572868
  57.9 8.6 %copy-start.21 = (bf16[32,16,512]{2,1,0:T(8,128)(2,1)S(1)}, bf16[32,16,512]{2,1,0:T(8,128)(2,1)}, u32[]{:S(2)}) copy-start(bf16[32,16,512]{2,1,0:T(8,128)(2,1)} %param.25) | copy-start | bytes 1572868
  58.5 7.8 %copy-start.8 = (bf16[32,16,512]{2,0,1:T(8,128)(2,1)}, bf16[32,16,512]{2,0,1:T(8,128)(2,1)S(1)}, u32[]{:S(2)}) copy-start(bf16[32,16,512]{2,0,1:T(8,128)(2,1)S(1)} %fusion.54) | copy-start | bytes 1572868
  123.3 53.7 %copy-start.50 = (s32[32]{0:T(128)S(1)}, s32[32]{0:T(128)}, u32[]{:S(2)}) copy-start(s32[32]{0:T(128)} %param.30) | copy-start | bytes 388
  176.9 6.6 %copy-start.3 = (bf16[32,16,512]{2,1,0:T(8,128)(2,1)S(1)}, bf16[32,16,512]{2,1,0:T(8,128)(2,1)}, u32[]{:S(2)}) copy-start(bf16[32,16,512]{2,1,0:T(8,128)(2,1)} %param.24) | copy-start | bytes 1572868
  176.9 6.6 %copy-start.22 = (bf16[32,16,512]{2,1,0:T(8,128)(2,1)S(1)}, bf16[32,16,512]{2,1,0:T(8,128)(2,1)}, u32[]{:S(2)}) copy-start(bf16[32,16,512]{2,1,0:T(8,128)(2,1)} %param.25) | copy-start | bytes 1572868
  176.9 6.6 %copy-start.55 = (f32[32]{0:T(128)S(1)}, f32[32]{0:T(128)}, u32[]{:S(2)}) copy-start(f32[32]{0:T(128)} %copy-done.54) | copy-start | bytes 388
  259.4 9.8 %copy-start.12 = (bf16[32,16,512]{2,0,1:T(8,128)(2,1)S(1)}, bf16[32,16,512]{2,0,1:T(8,128)(2,1)}, u32[]{:S(2)}) copy-start(bf16[32,16,512]{2,0,1:T(8,128)(2,1)} %copy-done.11) | copy-start | bytes 1572868
  259.4 9.8 %copy-start.28 = (bf16[32,16,512]{2,0,1:T(8,128)(2,1)S(1)}, bf16[32,16,512]{2,0,1:T(8,128)(2,1)}, u32[]{:S(2)}) copy-start(bf16[32,16,512]{2,0,1:T(8,128)(2,1)} %copy-done.27) | copy-start | bytes 1572868
  260.8 29.2 %copy-start.13 = (bf16[32,16,512]{2,0,1:T(8,128)(2,1)}, bf16[32,16,512]{2,0,1:T(8,128)(2,1)S(1)}, u32[]{:S(2)}) copy-start(bf16[32,16,512]{2,0,1:T(8,128)(2,1)S(1)} %copy.162) | copy-start | bytes 1572868
  263.3 9.3 %copy-start.41 = (f32[32,512]{1,0:T(8,128)S(1)}, f32[32,512]{1,0:T(8,128)}, u32[]{:S(2)}) copy-start(f32[32,512]{1,0:T(8,128)} %get-tuple-element.633) | copy-start | bytes 196612
  263.3 9.3 %copy-start.51 = (s32[32]{0:T(128)S(1)}, s32[32]{0:T(128)}, u32[]{:S(2)}) copy-start(s32[32]{0:T(128)} %param.30) | copy-start | bytes 388
  265.5 7.4 %copy-start.20 = (bf16[4,32,4,512]{3,2,1,0:T(4,128)(2,1)S(1)}, bf16[4,32,4,512]{3,2,1,0:T(4,128)(2,1)}, u32[]{:S(2)}) copy-start(bf16[4,32,4,512]{3,2,1,0:T(4,128)(2,1)} %get-tuple-element.421) | copy-start | bytes 1572868
  290.0 17.4 %copy-start.16 = (bf16[2,64,2048]{2,1,0:T(8,128)(2,1)S(1)}, bf16[2,64,2048]{2,1,0:T(8,128)(2,1)}, u32[]{:S(2)}) copy-start(bf16[2,64,2048]{2,1,0:T(8,128)(2,1)} %param.33) | copy-start | bytes 1572868
  290.1 17.6 %copy-start.53 = (f32[128,8]{0,1:T(8,128)S(1)}, f32[128,8]{0,1:T(8,128)}, u32[]{:S(2)}) copy-start(f32[128,8]{0,1:T(8,128)} %copy-done.52) | copy-start | bytes 12292
  290.1 10.5 %slice-start = ((bf16[32,16,512]{2,0,1:T(8,128)(2,1)}), bf16[32,7,512]{2,0,1:T(8,128)(2,1)S(1)}, s32[]{:S(2)}) async-start(bf16[32,16,512]{2,0,1:T(8,128)(2,1)} %copy-done.13), calls=%async_computation.1 | async-start | bytes 458752 | tf_op jit(solution)/shard_map/transpose(jvp())/split | solution.py:21
  291.6 18.3 %copy-start.14 = (bf16[32,16,512]{2,0,1:T(8,128)(2,1)S(1)}, bf16[32,16,512]{2,0,1:T(8,128)(2,1)}, u32[]{:S(2)}) copy-start(bf16[32,16,512]{2,0,1:T(8,128)(2,1)} %copy-done.13) | copy-start | bytes 1572868
  292.4 18.9 %copy-start.1 = (f32[32,16,512]{2,0,1:T(8,128)S(1)}, f32[32,16,512]{2,0,1:T(8,128)}, u32[]{:S(2)}) copy-start(f32[32,16,512]{2,0,1:T(8,128)} %copy-done) | copy-start | bytes 3145732
  (40 other events, 148.3 us)
Sparse Core Ops, SparseCore 0:
  290.1 227.1 all-reduce.61
where the time goes:
time: 615 us; the launch traced here: 607 us
  waiting for transfers between devices  205 us (33%)
  other arithmetic  130 us (21%)
  local copies, waits for them, and re-layouts  110 us (18%)
  matrix products  73.2 us (12%)
  blocking collectives  64.5 us (10%)
  between operations  20.6 us (3%)
    unnamed x2, waiting for transfers between devices  205 us
    psum x1, blocking collectives, per_device(): lax.psum((first_term, local_squares), ('inner', 'outer'))  64.5 us
    dot_general x48, matrix products, mix(): jnp.dot(block, weight[order], preferred_element_type=jnp.float32)  63.7 us
    scatter-add x8, other arithmetic, slot_step(): source = jnp.take(lifted, index, axis=0).astype(jnp.float32)  40.9 us
    gather x16, local copies, waits for them, and re-layouts, slot_step(): source = jnp.take(lifted, index, axis=0).astype(jnp.float32)  27 us
    squeeze x32, local copies, waits for them, and re-layouts, interaction(): lax.scan(jax.checkpoint(slot_step), jnp.zeros((rows, feats.shape[1], widt...  26.7 us
    convert_element_type x24, other arithmetic, slot_step(): source = jnp.take(lifted, index, axis=0).astype(jnp.float32)  13.4 us
  transfers between devices with their start and end apart: 1, of which 1 were waited for; matrix products, arithmetic and copies ran while one was open for 4% of the time, Pallas kernels for 0%

commit v1 on v0

v1 whole, which is shorter than its diff:
```python
import functools

import jax
import jax.numpy as jnp
from jax import lax
from jax.experimental import pallas as pl
from jax.experimental.pallas import tpu as pltpu
from jax.sharding import PartitionSpec as P

MESH = pl.DeviceIdType.MESH
F32, BF16, I32 = jnp.float32, jnp.bfloat16, jnp.int32
HIGH = lax.Precision.HIGHEST
CLIP_NORM = 2048.0

LEVELS = ((0, 1), (1, 4), (4, 9), (9, 16))
ATOMS = 32
EDGES = 128
C = 512

MATS = (
    [("out", 1, d) for d in range(4)]
    + [("up", 1, d) for d in range(4)]
    + [("out", 0, d) for d in range(4)]
    + [("up", 0, d) for d in range(4)]
)
CLASS = [q % 3 for q in range(16)]
CLASS[14] = 1
SEC, GAIN = 16, 17
CLASS = CLASS + [2, 2]
NUNITS = 18
ORDER = ((2, 0, 1), (1, 2, 0), (0, 1, 2))
PAIRS = []
for _k in range(3):
    _own = [q for q in range(16) if CLASS[q] == _k]
    PAIRS += [(_own[n], _own[n + 1]) for n in range(0, len(_own), 2)]
NPAIRS = len(PAIRS)
D1, D2, D3 = 3, 6, 9
OUT_SLOTS = 4


def dot(a, b, precision=None):
    return lax.dot_general(
        a, b, (((1,), (0,)), ((), ())), precision=precision, preferred_element_type=F32
    )


def dot_nt(a, b, precision=None):
    return lax.dot_general(
        a, b, (((1,), (1,)), ((), ())), precision=precision, preferred_element_type=F32
    )


def position():
    inner, outer = lax.axis_index("inner"), lax.axis_index("outer")
    return inner // 2, inner % 2, outer // 4, outer % 4


def peer(axis, step):
    x, c, z, y = position()
    if axis == 0:
        x = (x + step) % 4
    elif axis == 1:
        z = (z + step) % 4
    elif axis == 2:
        y = (y + step) % 4
    else:
        c = 1 - c
    return (x * 2 + c, z * 4 + y)


def along(axis):
    x, c, z, y = position()
    return (x, z, y, c)[axis]


def rows_of(first, last):
    return slice(first * ATOMS, last * ATOMS)


def iota(shape, dim):
    return lax.broadcasted_iota(I32, shape, dim)


def onehot(mask):
    return jnp.where(mask, 1.0, 0.0).astype(BF16)


def kernel(
    counts, feat, cot, send, ang, basis, spec, w_first, gain, wup_h, wsec_h, wout_h,
    up_o, first_o, sec_o, out_o, gain_o, fg_o,
    wup, wout, wsec, wfp, gpad, wsem,
    xb, lg, rad, pre, hid, sm, mx, grow, abc, lbuf, dyb, dmx, dsb, dr, dl0, dsrc, dl, drt, xt, pt, dsk,
    own, own_s, own_g, outb, outb_s, outb_g,
    rx0, rx0_s, rx0_g, rx1, rx1_s, rx1_g, rx2, rx2_s, rx2_g,
    f2, f2_s, f2_g, s3, s3_s, s3_g, rx3, rx3_s, rx3_g, fin, fin_s, fin_g,
    red, redrx,
    ss0, rs0, ss1, rs1, ss2, rs2, ss3, rs3, ssr, rsr,
):
    x, c, z, y = position()

    loads = {}
    for layer in (0, 1):
        loads["up", layer] = pltpu.make_async_copy(wup_h.at[layer], wup.at[layer], wsem.at[3 * layer])
        loads["sec", layer] = pltpu.make_async_copy(
            wsec_h.at[layer], wsec.at[layer, pl.ds(64 * layer, 64)], wsem.at[3 * layer + 1]
        )
        loads["out", layer] = pltpu.make_async_copy(wout_h.at[layer], wout.at[layer], wsem.at[3 * layer + 2])
    for layer in (0, 1):
        for name in ("up", "sec", "out"):
            loads[name, layer].start()

    barrier = pltpu.get_barrier_semaphore()
    for axis in range(3):
        for step in (1, 2, 3):
            pl.semaphore_signal(barrier, inc=1, device_id=peer(axis, step), device_id_type=MESH)
    pl.semaphore_signal(barrier, inc=1, device_id=peer(3, 1), device_id_type=MESH)

    count = counts[0]
    r, cl = iota((C, C), 0), iota((C, C), 1)
    to_comp = onehot(cl == (r & 31) * 16 + (r >> 5))
    xb[0] = dot(to_comp, feat[...]).astype(BF16)
    to_comp_live = onehot((cl == (r & 31) * 16 + (r >> 5)) & ((r & 31) < count))
    dyb[...] = dot(to_comp_live, cot[...])
    for k in range(3):
        digits = ((r >> 6) & 3, (r >> 4) & 3, (r >> 2) & 3)
        held = {ORDER[k][n]: digits[n] for n in range(3)}
        source = held[0] * 128 + ((r >> 8) ^ c) * 64 + held[1] * 16 + held[2] * 4 + (r & 3)
        pt[k] = onehot(cl == source)
    eye = onehot(r == cl)
    pt[3] = eye
    eye_e = onehot(iota((EDGES, EDGES), 0) == iota((EDGES, EDGES), 1))
    row = jnp.concatenate([send[s : s + 1, :] for s in range(4)], axis=1)
    scatter = onehot(iota((ATOMS, EDGES), 0) == row)
    gather = dot_nt(eye_e, scatter).astype(BF16)
    ang2 = jnp.concatenate([ang[:, s, :] for s in range(4)], axis=1)
    basis2 = jnp.concatenate([basis[:, s, :] for s in range(4)], axis=1)
    ang_t = jnp.transpose(ang2)
    for m in range(16):
        abc[m] = jnp.broadcast_to(ang_t[:, m : m + 1], (EDGES, 128))
    basis_t = jnp.transpose(basis2)
    kind_t = onehot(iota((128, ATOMS), 0) == spec[...])
    eye_a = onehot(iota((ATOMS, ATOMS), 0) == iota((ATOMS, ATOMS), 1))
    kind = dot_nt(eye_a, kind_t)
    kind_b = kind.astype(BF16)
    wfp[...] = jnp.zeros_like(wfp)
    gpad[...] = jnp.zeros_like(gpad)
    for layer in (0, 1):
        wfp[layer, :, 64 * layer : 64 * layer + 64] = w_first[layer]
        gpad[layer, 0:89, :] = gain[layer]
        wsec[layer, 64 * (1 - layer) : 64 * (1 - layer) + 64, :] = jnp.zeros((64, 2048), BF16)
        grow[layer] = dot(kind, gpad[layer], HIGH)

    tiles = [(s, t) for t in range(4) for s in range(4)]

    def edge_rows(s):
        return pl.ds(s * ATOMS, ATOMS)

    def lanes(t):
        return pl.ds(t * 128, 128)

    for layer in (0, 1):
        loads["up", layer].wait()
        for d, (a, b) in enumerate(LEVELS):
            lbuf[rows_of(a, b), :] = dot(xb[layer, rows_of(a, b), :], wup[layer, d]).astype(BF16)
        loads["sec", layer].wait()
        p = dot(basis_t, wfp[layer], HIGH)
        pre[layer] = p
        hid[layer] = (p * jax.nn.sigmoid(p)).astype(BF16)
        for d in range(4):
            rad[layer, :, d * C : (d + 1) * C] = dot(hid[layer], wsec[layer, :, d * C : (d + 1) * C])

        for d, (a, b) in enumerate(LEVELS):

            def message(m, carry, d=d, layer=layer):
                at = pl.multiple_of(m * ATOMS, ATOMS)
                lg[layer, m] = dot(gather, lbuf[pl.ds(at, ATOMS), :]).astype(BF16)
                for t in range(4):
                    total = jnp.zeros((ATOMS, 128), F32)
                    for s in range(4):
                        src = lg[layer, m, edge_rows(s), lanes(t)].astype(F32)
                        src0 = lg[layer, 0, edge_rows(s), lanes(t)].astype(F32)
                        weight = rad[layer, edge_rows(s), pl.ds(d * C + t * 128, 128)]
                        total += weight * (abc[m, edge_rows(s), :] * src0 + src)
                    sm[layer, pl.ds(at, ATOMS), lanes(t)] = (total * 0.25).astype(BF16)
                return carry

            lax.fori_loop(a, b, message, 0)
        loads["out", layer].wait()
        for d, (a, b) in enumerate(LEVELS):
            mx[layer, rows_of(a, b), :] = dot(sm[layer, rows_of(a, b), :], wout[layer, d])
        if layer == 0:

            def gated(m, carry):
                at = pl.multiple_of(m * ATOMS, ATOMS)
                gate = jax.nn.sigmoid(mx[0, 0:ATOMS, :])
                value = mx[0, pl.ds(at, ATOMS), :] * gate
                value += grow[0] * xb[0, pl.ds(at, ATOMS), :].astype(F32)
                xb[1, pl.ds(at, ATOMS), :] = value.astype(BF16)
                return carry

            lax.fori_loop(0, 16, gated, 0)

    def bufs(u):
        if u == SEC:
            return own_s, outb_s, rx0_s, rx1_s, rx2_s, f2_s, 1024
        if u == GAIN:
            return own_g, outb_g, rx0_g, rx1_g, rx2_g, f2_g, 256
        return own.at[u], outb.at[u % OUT_SLOTS], rx0.at[u], rx1.at[u], rx2.at[u], f2.at[u], 256

    def step0(u):
        _, out_r, r0, _, _, _, _ = bufs(u)
        return pltpu.make_async_remote_copy(
            src_ref=out_r, dst_ref=r0, send_sem=ss0.at[u], recv_sem=rs0.at[u],
            device_id=peer(3, 1), device_id_type=MESH,
        )

    def chunk(ref, rows, which, part, parts):
        size = rows // 4 // parts
        return ref.at[pl.ds(pl.multiple_of(which * (rows // 4) + part * size, size), size)]

    def step1(u):
        o, _, _, r1, _, _, rows = bufs(u)
        axis = ORDER[CLASS[u]][0]
        p = along(axis)
        plan = (
            ((p + 2) % 4, 0, 1), ((p + 1) % 4, 1, 1),
            ((p + 2) % 4, 1, 3), ((p + 3) % 4, 0, 3),
            ((p + 1) % 4, 0, 1), ((p + 3) % 4, 1, 3),
        )
        return [
            pltpu.make_async_remote_copy(
                src_ref=chunk(o, rows, which, part, 2), dst_ref=r1.at[n],
                send_sem=ss1.at[6 * u + n], recv_sem=rs1.at[6 * u + n],
                device_id=peer(axis, way), device_id_type=MESH,
            )
            for n, (which, part, way) in enumerate(plan)
        ]

    def step2(u):
        o, _, _, _, r2, _, rows = bufs(u)
        first, second, _ = ORDER[CLASS[u]]
        p1, p2 = along(first), along(second)
        size = rows // 16
        return [
            pltpu.make_async_remote_copy(
                src_ref=o.at[pl.ds(pl.multiple_of(p1 * (rows // 4) + ((p2 + j) % 4) * size, size), size)],
                dst_ref=r2.at[j - 1],
                send_sem=ss2.at[3 * u + j - 1], recv_sem=rs2.at[3 * u + j - 1],
                device_id=peer(second, j), device_id_type=MESH,
            )
            for j in (1, 2, 3)
        ]

    def step3(n):
        if n < NPAIRS:
            k, src, dst = CLASS[PAIRS[n][0]], s3.at[n], rx3.at[n]
        elif n == NPAIRS:
            k, src, dst = 2, s3_s, rx3_s
        else:
            k, src, dst = 2, s3_g, rx3_g
        axis = ORDER[k][2]
        p = along(axis)
        return [
            pltpu.make_async_remote_copy(
                src_ref=src.at[(p + j) % 4], dst_ref=dst.at[j - 1],
                send_sem=ss3.at[3 * n + j - 1], recv_sem=rs3.at[3 * n + j - 1],
                device_id=peer(axis, j), device_id_type=MESH,
            )
            for j in (1, 2, 3)
        ]

    sent = []

    def start(copies):
        for one in copies:
            one.start()
            sent.append(one)

    done2 = set()

    def service(tick):
        u = tick
        if u < NUNITS:
            start([step0(u)])
        u = tick - 1
        if 0 <= u < NUNITS:
            o, _, r0, _, _, _, rows = bufs(u)
            step0(u).wait_recv()
            o[...] = o[...] + r0[...]
            start(step1(u)[:4])
        u = tick - D1
        if 0 <= u < NUNITS:
            o, _, _, r1, _, _, rows = bufs(u)
            copies = step1(u)
            p = along(ORDER[CLASS[u]][0])
            for first, second, which, part in ((0, 4, (p + 1) % 4, 0), (2, 5, (p + 3) % 4, 1)):
                copies[first].wait_recv()
                view = chunk(o, rows, which, part, 2)
                view[...] = view[...] + r1[first]
                start([copies[second]])
        u = tick - D2
        if 0 <= u < NUNITS:
            o, _, _, r1, _, _, rows = bufs(u)
            copies = step1(u)
            p = along(ORDER[CLASS[u]][0])
            for direct, summed, part in ((3, 4, 0), (1, 5, 1)):
                copies[direct].wait_recv()
                copies[summed].wait_recv()
                view = chunk(o, rows, p, part, 2)
                view[...] = view[...] + r1[direct] + r1[summed]
            start(step2(u))
        u = tick - D3
        if 0 <= u < NUNITS:
            o, _, _, _, r2, ff, rows = bufs(u)
            first, second, _ = ORDER[CLASS[u]]
            for copy in step2(u):
                copy.wait_recv()
            size = rows // 16
            at = pl.multiple_of(along(first) * (rows // 4) + along(second) * size, size)
            value = o[pl.ds(at, size)] + r2[0] + r2[1] + r2[2]
            if u == SEC:
                for n in range(4):
                    s3_s[n] = value[16 * n : 16 * n + 16]
                start(step3(NPAIRS))
            elif u == GAIN:
                for n in range(4):
                    s3_g[n] = jnp.concatenate(
                        [value[4 * n : 4 * n + 4, 0:128], value[4 * n : 4 * n + 4, 128:256]], axis=0
                    )
                start(step3(NPAIRS + 1))
            else:
                ff[...] = value
                done2.add(u)
                for n, (ua, ub) in enumerate(PAIRS):
                    if u in (ua, ub) and ua in done2 and ub in done2:
                        va, vb = f2[ua], f2[ub]
                        for q in range(4):
                            s3[n, q] = jnp.concatenate([va[4 * q : 4 * q + 4], vb[4 * q : 4 * q + 4]], axis=0)
                        start(step3(n))

    def put(u, a, g):
        rows = a.shape[0]
        xt[:, 0:rows] = dot_nt(pt[CLASS[u]], a).astype(BF16)
        if u >= OUT_SLOTS:
            step0(u - OUT_SLOTS).wait_send()
        o, out_r = bufs(u)[:2]
        o[...] = dot(xt[0:256, 0:rows], g)
        out_r[...] = dot(xt[256:512, 0:rows], g)

    waited_barrier = False
    tick = 0
    for layer in (1, 0):
        t = mx[layer, 0:ATOMS, :]
        gate = jax.nn.sigmoid(t)
        dy0 = dyb[0:ATOMS, :]

        def gates(m, carry, layer=layer, gate=gate):
            dgate, dskip = carry
            at = pl.ds(pl.multiple_of(m * ATOMS, ATOMS), ATOMS)
            dy = dyb[at, :]
            dmx[at, :] = (dy * gate).astype(BF16)
            dgate += dy * mx[layer, at, :]
            dskip += dy * xb[layer, at, :].astype(F32)
            return dgate, dskip

        zero = jnp.zeros((ATOMS, C), F32)
        dgate, dskip = lax.fori_loop(
            1, 16, gates, (zero, dy0 * xb[layer, 0:ATOMS, :].astype(F32))
        )
        slope = gate * (1.0 - gate)
        dmx[0:ATOMS, :] = (dy0 * (gate + t * slope) + dgate * slope).astype(BF16)
        dsk[layer] = dskip

        if not waited_barrier:
            pl.semaphore_wait(barrier, 10)
            waited_barrier = True
        for d, (a, b) in enumerate(LEVELS):
            put(tick, sm[layer, rows_of(a, b), :], dmx[rows_of(a, b), :])
            service(tick)
            tick += 1
        for d, (a, b) in enumerate(LEVELS):
            dsb[rows_of(a, b), :] = dot_nt(dmx[rows_of(a, b), :], wout[layer, d]) * 0.25

        dr[...] = jnp.zeros_like(dr)
        dl0[...] = jnp.zeros_like(dl0)
        for d, (a, b) in enumerate(LEVELS):

            def back(m, carry, d=d, layer=layer, lone=(d == 0)):
                at = pl.multiple_of(m * ATOMS, ATOMS)
                for t in range(4):
                    dt = dsb[pl.ds(at, ATOMS), lanes(t)]
                    for s in range(4):
                        src = lg[layer, m, edge_rows(s), lanes(t)].astype(F32)
                        src0 = lg[layer, 0, edge_rows(s), lanes(t)].astype(F32)
                        wide = pl.ds(d * C + t * 128, 128)
                        weight = rad[layer, edge_rows(s), wide]
                        harm = abc[m, edge_rows(s), :]
                        q = dt * weight
                        dr[edge_rows(s), wide] += dt * (harm * src0 + src)
                        if lone:
                            dl0[edge_rows(s), lanes(t)] += q + harm * q
                        else:
                            dl0[edge_rows(s), lanes(t)] += harm * q
                            dsrc[edge_rows(s), lanes(t)] = q.astype(BF16)
                if not lone:
                    dl[pl.ds(at, ATOMS), :] = dot(scatter, dsrc[...]).astype(BF16)
                return carry

            if d == 0:
                back(0, 0)
            else:
                lax.fori_loop(a, b, back, 0)
        dl[0:ATOMS, :] = dot(scatter, dl0[...].astype(BF16)).astype(BF16)

        for d, (a, b) in enumerate(LEVELS):
            put(tick, xb[layer, rows_of(a, b), :], dl[rows_of(a, b), :])
            service(tick)
            tick += 1
        for d, (a, b) in enumerate(LEVELS):
            dsb[rows_of(a, b), :] = dot_nt(dl[rows_of(a, b), :], wup[layer, d])

        def skip(m, carry, layer=layer):
            at = pl.ds(pl.multiple_of(m * ATOMS, ATOMS), ATOMS)
            dyb[at, :] = dsb[at, :] + grow[layer] * dyb[at, :]
            return carry

        lax.fori_loop(0, 16, skip, 0)
        drb = dr[...].astype(BF16)
        for d in range(4):
            drt[layer, d] = dot_nt(pt[3], drb[:, d * C : (d + 1) * C]).astype(BF16)
        dhid = dot_nt(drb, wsec[layer])
        p = pre[layer]
        sg = jax.nn.sigmoid(p)
        dpre = dhid * (sg * (1.0 + p * (1.0 - sg)))
        term = dot(basis2, dpre, HIGH)
        if layer == 1:
            red[0] = term
        else:
            red[0] = red[0] + term

    for d in range(4):
        blk = dot(drt[0, d], hid[0]) + dot(drt[1, d], hid[1])
        for half in range(2):
            part = blk[256 * half : 256 * half + 256]
            @pl.when(c == half)
            def _(part=part, d=d):
                own_s[256 * d : 256 * d + 256, :] = part

            @pl.when(c != half)
            def _(part=part, d=d):
                outb_s[256 * d : 256 * d + 256, :] = part

    service(tick)
    tick += 1
    for layer in (0, 1):
        hi = dsk[layer].astype(BF16)
        lo = (dsk[layer] - hi.astype(F32)).astype(BF16)
        blk = dot(dot_nt(pt[2], hi).astype(BF16), kind_b) + dot(dot_nt(pt[2], lo).astype(BF16), kind_b)
        own_g[:, 128 * layer : 128 * layer + 128] = blk[0:256]
        outb_g[:, 128 * layer : 128 * layer + 128] = blk[256:512]
    service(tick)
    tick += 1

    to_atom = onehot(cl == (r & 15) * 32 + (r >> 4))
    fg_o[...] = dot(to_atom, dyb[...].astype(BF16)).astype(BF16)

    def all_sum(which, stage):
        axis = stage
        n = 2 if axis == 3 else 4
        p = along(axis)
        base = (which * 4 + stage) * 4
        copies = [
            pltpu.make_async_remote_copy(
                src_ref=red.at[which * 5 + stage], dst_ref=redrx.at[base + p],
                send_sem=ssr.at[base + j], recv_sem=rsr.at[base + p],
                device_id=peer(axis, j), device_id_type=MESH,
            )
            for j in range(1, n)
        ]
        waits = [
            pltpu.make_async_remote_copy(
                src_ref=red.at[which * 5 + stage], dst_ref=redrx.at[base + (p + j) % n],
                send_sem=ssr.at[base + j], recv_sem=rsr.at[base + (p + j) % n],
                device_id=peer(axis, j), device_id_type=MESH,
            )
            for j in range(1, n)
        ]
        return copies, waits, base, n, p

    def all_sum_start(which, stage):
        copies, _, base, n, p = all_sum(which, stage)
        start(copies)
        redrx[base + p] = red[which * 5 + stage]

    def all_sum_end(which, stage):
        _, waits, base, n, p = all_sum(which, stage)
        for one in waits:
            one.wait_recv()
        value = redrx[base]
        for j in range(1, n):
            value = value + redrx[base + j]
        red[which * 5 + stage + 1] = value

    all_sum_start(0, 0)
    stage = 0
    while tick < NUNITS + D3:
        service(tick)
        tick += 1
        if stage < 4 and tick % 2 == 0:
            all_sum_end(0, stage)
            stage += 1
            if stage < 4:
                all_sum_start(0, stage)

    squares = jnp.zeros((8, 128), F32)
    for n in range(NPAIRS + 2):
        if n < NPAIRS:
            src, rec, out, k = s3.at[n], rx3.at[n], fin.at[n], CLASS[PAIRS[n][0]]
        elif n == NPAIRS:
            src, rec, out, k = s3_s, rx3_s, fin_s, 2
        else:
            src, rec, out, k = s3_g, rx3_g, fin_g, 2
        for copy in step3(n):
            copy.wait_recv()
        value = src[along(ORDER[k][2])] + rec[0] + rec[1] + rec[2]
        out[...] = value
        sq = value * value
        if n < NPAIRS:
            for q in range(4):
                squares += sq[:, 128 * q : 128 * q + 128]
        elif n == NPAIRS:
            squares += sq[0:8] + sq[8:16]
        else:
            squares += sq
    red[5] = squares
    for stage in range(4):
        all_sum_start(1, stage)
        all_sum_end(1, stage)
    first_sum = red[4]
    total = jnp.sum(jnp.sum(red[9] + first_sum * first_sum, axis=1, keepdims=True), axis=0, keepdims=True)
    scale = jnp.minimum(1.0, CLIP_NORM / jnp.sqrt(total + 1e-6))

    for n, pair in enumerate(PAIRS):
        value = fin[n] * scale
        for half, u in enumerate(pair):
            which, layer, d = MATS[u]
            ref = up_o if which == "up" else out_o
            ref[layer, d] = value[4 * half : 4 * half + 4]
    scaled = first_sum * scale
    first_o[0] = scaled[:, 0:64]
    first_o[1] = scaled[:, 64:128]
    sec_t = jnp.transpose(fin_s[...] * scale)
    sec_o[0] = sec_t[0:64]
    sec_o[1] = sec_t[64:128]
    gain_t = jnp.transpose(fin_g[...] * scale)
    gain_o[0] = gain_t[0:89, 0:4]
    gain_o[1] = gain_t[0:89, 4:8]

    waited = set(range(0, NUNITS))
    for one in sent:
        pass
    for u in range(NUNITS):
        if not (u < 16 and u + OUT_SLOTS < 16):
            step0(u).wait_send()
        for copy in step1(u) + step2(u):
            copy.wait_send()
    for n in range(NPAIRS + 2):
        for copy in step3(n):
            copy.wait_send()
    for which in range(2):
        for stage in range(4):
            for copy in all_sum(which, stage)[0]:
                copy.wait_send()


def per_device(features, cotangent, counts, senders, angular, basis, species, w_up, w_first, w_second, w_out, gain):
    vm, hbm = pl.BlockSpec(memory_space=pltpu.VMEM), pl.BlockSpec(memory_space=pl.ANY)
    V = pltpu.VMEM
    dma = pltpu.SemaphoreType.DMA
    scratch = [
        V((2, 4, C, C), BF16), V((2, 4, C, C), BF16), V((2, 128, 2048), BF16), V((2, 8, 128), F32), V((2, 128, C), F32), dma((6,)),
        V((2, C, C), BF16),
        V((2, 16, EDGES, C), BF16),
        V((2, EDGES, 2048), F32),
        V((2, EDGES, 128), F32),
        V((2, EDGES, 128), BF16),
        V((2, C, C), BF16),
        V((2, C, C), F32),
        V((2, ATOMS, C), F32),
        V((16, EDGES, 128), F32),
        V((C, C), BF16),
        V((C, C), F32),
        V((C, C), BF16),
        V((C, C), F32),
        V((EDGES, 2048), F32),
        V((EDGES, C), F32),
        V((EDGES, C), BF16),
        V((C, C), BF16),
        V((2, 4, C, EDGES), BF16),
        V((C, 256), BF16),
        V((4, C, C), BF16),
        V((2, ATOMS, C), F32),
        V((16, 256, C), F32), V((1024, 128), F32), V((256, 256), F32),
        V((OUT_SLOTS, 256, C), F32), V((1024, 128), F32), V((256, 256), F32),
        V((16, 256, C), F32), V((1024, 128), F32), V((256, 256), F32),
        V((16, 6, 32, C), F32), V((6, 128, 128), F32), V((6, 32, 256), F32),
        V((16, 3, 16, C), F32), V((3, 64, 128), F32), V((3, 16, 256), F32),
        V((16, 16, C), F32), V((64, 128), F32), V((16, 256), F32),
        V((NPAIRS, 4, 8, C), F32), V((4, 16, 128), F32), V((4, 8, 128), F32),
        V((NPAIRS, 3, 8, C), F32), V((3, 16, 128), F32), V((3, 8, 128), F32),
        V((NPAIRS, 8, C), F32), V((16, 128), F32), V((8, 128), F32),
        V((10, 8, 128), F32), V((32, 8, 128), F32),
        dma((NUNITS,)), dma((NUNITS,)), dma((6 * NUNITS,)), dma((6 * NUNITS,)),
        dma((3 * NUNITS,)), dma((3 * NUNITS,)), dma((3 * (NPAIRS + 2),)), dma((3 * (NPAIRS + 2),)),
        dma((32,)), dma((32,)),
    ]
    shape = jax.ShapeDtypeStruct
    up, first, second, out, gain_grad, feature_grad = pl.pallas_call(
        kernel,
        name="interaction_grads",
        out_shape=(
            shape((2, 4, 4, C), F32), shape((2, 8, 64), F32), shape((2, 64, 16), F32),
            shape((2, 4, 4, C), F32), shape((2, 89, 4), F32), shape((C, C), BF16),
        ),
        in_specs=[pl.BlockSpec(memory_space=pltpu.SMEM)] + [vm] * 8 + [hbm] * 3,
        out_specs=(vm,) * 6,
        scratch_shapes=scratch,
        compiler_params=pltpu.CompilerParams(
            collective_id=0, has_side_effects=True, vmem_limit_bytes=63 * 2**20
        ),
        cost_estimate=pl.CostEstimate(flops=8 * 10**9, bytes_accessed=12 * 10**6, transcendentals=10**5),
    )(
        counts, features.reshape(C, C), cotangent.reshape(C, C), senders, angular, basis,
        species.reshape(1, ATOMS), w_first, gain, w_up, w_second, w_out,
    )
    return up, first, second, out, gain_grad, feature_grad.reshape(features.shape)


def solution(mesh):
    both = ("inner", "outer")
    return jax.shard_map(
        per_device,
        mesh=mesh,
        in_specs=(
            P(both, None, None), P(both, None, None), P(both), P(None, both), P(None, None, both),
            P(None, None, both), P(both), P(), P(), P(), P(), P(),
        ),
        out_specs=(
            P(None, None, both, None), P(), P(None, None, both), P(None, None, both, None),
            P(None, None, both), P(both, None, None),
        ),
        check_vma=False,
    )
```

time: 615 us -> 114 us (0.19); the launches traced: 607 us -> 114 us
  waiting for transfers between devices: 205 us -> 0 us
  other arithmetic: 130 us -> 0 us
  Pallas kernels: 0 us -> 102 us
  local copies, waits for them, and re-layouts: 110 us -> 11 us
  matrix products: 73.2 us -> 0 us
  blocking collectives: 64.5 us -> 0 us
  between operations: 20.6 us -> 1.29 us
    unnamed x2 -> x0, waiting for transfers between devices: 205 us -> none
    pallas_call x0 -> x1, Pallas kernels: none -> 102 us  [per_device(): pl.pallas_call(kernel, name='interaction_grads', out_shape=(shape((2, 4,...]
    dot_general x62 -> x0, matrix products: 73.2 us -> none  [the longest x48 63.7 us: mix(): jnp.dot(block, weight[order], preferred_element_type=jnp.float32)]
    psum x1 -> x0, blocking collectives: 64.5 us -> none  [per_device(): lax.psum((first_term, local_squares), ('inner', 'outer'))]
    scatter-add x8 -> x0, other arithmetic: 40.9 us -> none  [slot_step(): source = jnp.take(lifted, index, axis=0).astype(jnp.float32)]
    gather x16 -> x0, local copies, waits for them, and re-layouts: 27 us -> none  [slot_step(): source = jnp.take(lifted, index, axis=0).astype(jnp.float32)]
    squeeze x32 -> x0, local copies, waits for them, and re-layouts: 26.7 us -> none  [interaction(): lax.scan(jax.checkpoint(slot_step), jnp.zeros((rows, feats.shape[1], widt...]
    convert_element_type x30 -> x0, other arithmetic: 22.5 us -> none  [the longest x24 13.4 us: slot_step(): source = jnp.take(lifted, index, axis=0).astype(jnp.float32)]
  transfers between devices with their start and end apart: 1 -> 0, of which waited for: 1 -> 0; matrix products, arithmetic and copies ran while one was open for 4% -> 0% of each run, Pallas kernels for 0% -> 0%
where the time goes in v1:
time: 114 us
  Pallas kernels  102 us (89%)
  local copies, waits for them, and re-layouts  11 us (10%)
  between operations  1.29 us (1%)
    pallas_call x1, Pallas kernels, per_device(): pl.pallas_call(kernel, name='interaction_grads', out_shape=(shape((2, 4,...  102 us
    unnamed x7, local copies, waits for them, and re-layouts  11 us

profile of v1, /device:TPU:1, one launch (start us, length us, event | category | flops | bytes accessed | tf_op | source)
XLA Modules:
  0.0 114.0 jit_solution(8198663533311217977)
XLA Ops:
  1.3 1.8 %copy.18.gain = f32[2,89,512]{2,1,0:T(8,128)} copy(f32[2,89,512]{2,0,1:T(2,128)} %param.23) | data formatting | bytes 729088 | tf_op args[11]
  3.1 101.7 %interaction_grads.1 = (f32[2,4,4,512]{3,2,1,0:T(4,128)}, f32[2,8,64]{2,1,0:T(8,128)}, f32[2,64,16]{2,1,0:T(8,128)}, f32[2,4,4,512]{3,2,1,0:T(4,128)}, f32[2,89,4]{2,1,0:T(8,128)}, /*index=5*/bf16[512,512]{1,0:T(8,128)(2,1)}) custom-call(s32[1]{0:T(128)S(6)} %copy.25.counts, bf16[512,512]{1,0:T(8,128)(2,1)} %bitcast.5, bf16[512,512]{1,0:T(8,128)(2,1)} %bitcast.6, ...), custom_call_target="tpu_custom_call" | custom-call | flops 8000000000 | bytes 12000000 | tf_op jit(solution)/shard_map/interaction_grads/pallas_call | solution.py:618
  104.8 1.6 %copy.20 = f32[2,89,4]{1,2,0:T(4,128)} copy(f32[2,89,4]{2,1,0:T(8,128)} %get-tuple-element.22) | data formatting | bytes 5696
  106.3 1.5 %copy.19 = f32[2,64,16]{1,2,0:T(8,128)} copy(f32[2,64,16]{2,1,0:T(8,128)} %get-tuple-element.20) | data formatting | bytes 16384
  107.8 1.5 %copy.26 = f32[2,4,4,512]{3,2,1,0:T(4,128)} copy(f32[2,4,4,512]{3,2,1,0:T(4,128)} %get-tuple-element.30) | data formatting | bytes 131072
  109.3 1.3 %copy.27 = f32[2,8,64]{2,1,0:T(8,128)} copy(f32[2,8,64]{2,1,0:T(8,128)} %get-tuple-element.31) | data formatting | bytes 8192
  110.6 1.5 %copy.28 = f32[2,4,4,512]{3,2,1,0:T(4,128)} copy(f32[2,4,4,512]{3,2,1,0:T(4,128)} %get-tuple-element.33) | data formatting | bytes 131072
  112.1 1.9 %copy.29 = bf16[32,16,512]{2,1,0:T(8,128)(2,1)} copy(bf16[32,16,512]{2,1,0:T(8,128)(2,1)} %bitcast.4) | data formatting | bytes 1048576

commit v2 on v1

v2 whole, which is shorter than its diff:
```python
import functools

import jax
import jax.numpy as jnp
from jax import lax
from jax.experimental import pallas as pl
from jax.experimental.pallas import tpu as pltpu
from jax.sharding import PartitionSpec as P

MESH = pl.DeviceIdType.MESH
F32, BF16, I32 = jnp.float32, jnp.bfloat16, jnp.int32
HIGH = lax.Precision.HIGHEST
CLIP_NORM = 2048.0

LEVELS = ((0, 1), (1, 4), (4, 9), (9, 16))
ATOMS = 32
EDGES = 128
C = 512

MATS = (
    [("out", 1, d) for d in range(4)]
    + [("up", 1, d) for d in range(4)]
    + [("out", 0, d) for d in range(4)]
    + [("up", 0, d) for d in range(4)]
)
CLASS = [q % 3 for q in range(16)]
CLASS[14] = 1
SEC, GAIN = 16, 17
CLASS = CLASS + [2, 2]
NUNITS = 18
ORDER = ((2, 0, 1), (1, 2, 0), (0, 1, 2))
PAIRS = []
for _k in range(3):
    _own = [q for q in range(16) if CLASS[q] == _k]
    PAIRS += [(_own[n], _own[n + 1]) for n in range(0, len(_own), 2)]
NPAIRS = len(PAIRS)
D0, D1, D2, D3 = 2, 6, 10, 13
OUT_SLOTS = 4


def dot(a, b, precision=None):
    return lax.dot_general(
        a, b, (((1,), (0,)), ((), ())), precision=precision, preferred_element_type=F32
    )


def dot_nt(a, b, precision=None):
    return lax.dot_general(
        a, b, (((1,), (1,)), ((), ())), precision=precision, preferred_element_type=F32
    )


GROUPS = ((0, 8), (1, 16))


def position():
    inner, outer = lax.axis_index("inner"), lax.axis_index("outer")
    return inner // 2, inner % 2, outer // 4, outer % 4


def peer(axis, step):
    x, c, z, y = position()
    if axis == 0:
        x = (x + step) % 4
    elif axis == 1:
        z = (z + step) % 4
    elif axis == 2:
        y = (y + step) % 4
    else:
        c = 1 - c
    return (x * 2 + c, z * 4 + y)


def group_peer(stage, step):
    inner, outer = lax.axis_index("inner"), lax.axis_index("outer")
    if stage == 0:
        return ((inner + step) % 8, outer)
    return (inner, (outer + step) % 16)


def along(axis):
    x, c, z, y = position()
    return (x, z, y, c)[axis]


def rows_of(first, last):
    return slice(first * ATOMS, last * ATOMS)


def iota(shape, dim):
    return lax.broadcasted_iota(I32, shape, dim)


def onehot(mask):
    return jnp.where(mask, 1.0, 0.0).astype(BF16)


def kernel(
    counts, send, ang, basis, spec, w_first, feat_h, cot_h, gain_h, wup_h, wsec_h, wout_h,
    fin, fin_s, fin_g, sums, fg_o,
    feat, cot, gain, wup, wout, wsec, wfp, gpad, wsem,
    xb, lg, rad, pre, hid, sm, mx, grow, abc, lbuf, dyb, dmx, dsb, dr, dl, drt, xt, pt, dsk, fgb,
    own, own_s, own_g, outb, outb_s, outb_g,
    rx0, rx0_s, rx0_g, rx1, rx1_s, rx1_g, rx2, rx2_s, rx2_g,
    f2, f2_s, f2_g, s3, s3_s, s3_g, rx3, rx3_s, rx3_g,
    red, redrx,
    ss0, rs0, ss1, rs1, ss2, rs2, ss3, rs3, ssr, rsr,
):
    x, c, z, y = position()

    loads = {}
    for layer in (0, 1):
        loads["up", layer] = pltpu.make_async_copy(wup_h.at[layer], wup.at[layer], wsem.at[3 * layer])
        loads["sec", layer] = pltpu.make_async_copy(
            wsec_h.at[layer], wsec.at[layer, pl.ds(64 * layer, 64)], wsem.at[3 * layer + 1]
        )
        loads["out", layer] = pltpu.make_async_copy(wout_h.at[layer], wout.at[layer], wsem.at[3 * layer + 2])
    for n, (name, src, dst) in enumerate((("feat", feat_h, feat), ("gain", gain_h, gain), ("cot", cot_h, cot))):
        loads[name] = pltpu.make_async_copy(src, dst, wsem.at[7 + n])
    for name in ("feat", ("up", 0), ("sec", 0), "gain", ("out", 0), ("up", 1), ("sec", 1), ("out", 1), "cot"):
        loads[name].start()

    barrier = pltpu.get_barrier_semaphore()
    for stage, n in GROUPS:
        for j in range(1, n):
            pl.semaphore_signal(barrier, inc=1, device_id=group_peer(stage, j), device_id_type=MESH)

    count = counts[0]
    r = iota((C, 128), 0)
    lane = iota((C, 128), 1)

    def picks(source):
        return jnp.concatenate([onehot(lane + 128 * t == source) for t in range(4)], axis=1)

    comp = (r & 31) * 16 + (r >> 5)
    to_comp = picks(comp)
    loads["feat"].wait()
    xb[0] = dot(to_comp, feat[...]).astype(BF16)

    made = set()

    def order_of(k):
        if k not in made:
            made.add(k)
            if k == 3:
                pt[k] = picks(r ^ (c << 8))
            else:
                digits = ((r >> 6) & 3, (r >> 4) & 3, (r >> 2) & 3)
                held = {ORDER[k][n]: digits[n] for n in range(3)}
                pt[k] = picks(held[0] * 128 + ((r >> 8) ^ c) * 64 + held[1] * 16 + held[2] * 4 + (r & 3))
        return pt[k]

    eye_e = onehot(iota((EDGES, EDGES), 0) == iota((EDGES, EDGES), 1))
    row = jnp.concatenate([send[s : s + 1, :] for s in range(4)], axis=1)
    scatter = onehot(iota((ATOMS, EDGES), 0) == row)
    gather = dot_nt(eye_e, scatter).astype(BF16)
    ang2 = jnp.concatenate([ang[:, s, :] for s in range(4)], axis=1)
    basis2 = jnp.concatenate([basis[:, s, :] for s in range(4)], axis=1)
    ang_t = jnp.transpose(ang2)
    for m in range(16):
        abc[m] = jnp.broadcast_to(ang_t[:, m : m + 1], (EDGES, 128))
    basis_t = jnp.transpose(basis2)
    wfp[...] = jnp.zeros_like(wfp)
    for layer in (0, 1):
        wfp[layer, :, 64 * layer : 64 * layer + 64] = w_first[layer]
        wsec[layer, 64 * (1 - layer) : 64 * (1 - layer) + 64, :] = jnp.zeros((64, 2048), BF16)

    def edge_rows(s):
        return pl.ds(s * ATOMS, ATOMS)

    def comp_rows(m):
        return pl.ds(m * ATOMS, ATOMS)

    def lanes(t, base=0):
        return pl.ds(pl.multiple_of(base + t * 128, 128), 128)

    def each_tile(body):
        def step(t, carry):
            body(t)
            return carry

        lax.fori_loop(0, 4, step, 0)

    for layer in (0, 1):
        loads["sec", layer].wait()
        p = dot(basis_t, wfp[layer], HIGH)
        pre[layer] = p
        hid[layer] = (p * jax.nn.sigmoid(p)).astype(BF16)
        for d in range(4):
            rad[layer, :, d * C : (d + 1) * C] = dot(hid[layer], wsec[layer, :, d * C : (d + 1) * C])
        loads["up", layer].wait()
        for d, (a, b) in enumerate(LEVELS):
            lbuf[rows_of(a, b), :] = dot(xb[layer, rows_of(a, b), :], wup[layer, d]).astype(BF16)
        for m in range(16):
            lg[layer, m] = dot(gather, lbuf[comp_rows(m), :]).astype(BF16)

        def message(t, layer=layer):
            src0 = [lg[layer, 0, edge_rows(s), lanes(t)].astype(F32) for s in range(4)]
            for d, (a, b) in enumerate(LEVELS):
                weight = [rad[layer, edge_rows(s), lanes(t, d * C)] for s in range(4)]
                from0 = [weight[s] * src0[s] for s in range(4)]
                for m in range(a, b):
                    total = jnp.zeros((ATOMS, 128), F32)
                    for s in range(4):
                        src = lg[layer, m, edge_rows(s), lanes(t)].astype(F32)
                        total += abc[m, edge_rows(s), :] * from0[s] + weight[s] * src
                    sm[layer, comp_rows(m), lanes(t)] = (total * 0.25).astype(BF16)

        each_tile(message)
        loads["out", layer].wait()
        for d, (a, b) in enumerate(LEVELS):
            mx[layer, rows_of(a, b), :] = dot(sm[layer, rows_of(a, b), :], wout[layer, d])
        if layer == 0:
            kind_t = onehot(iota((128, ATOMS), 0) == spec[...])
            eye_a = onehot(iota((ATOMS, ATOMS), 0) == iota((ATOMS, ATOMS), 1))
            kind = dot_nt(eye_a, kind_t)
            kind_b = kind.astype(BF16)
            gpad[...] = jnp.zeros_like(gpad)
            loads["gain"].wait()
            for k in (0, 1):
                gpad[k, 0:89, :] = gain[:, k, :]
                grow[k] = dot(kind, gpad[k], HIGH)

            def gated(t):
                gate = jax.nn.sigmoid(mx[0, 0:ATOMS, lanes(t)])
                skip_gain = grow[0, :, lanes(t)]
                for m in range(16):
                    value = mx[0, comp_rows(m), lanes(t)] * gate
                    value += skip_gain * xb[0, comp_rows(m), lanes(t)].astype(F32)
                    xb[1, comp_rows(m), lanes(t)] = value.astype(BF16)

            each_tile(gated)
    to_comp_live = picks(jnp.where((r & 31) < count, comp, -1))
    loads["cot"].wait()
    dyb[...] = dot(to_comp_live, cot[...])

    def bufs(u):
        if u == SEC:
            return own_s, outb_s, rx0_s, rx1_s, rx2_s, f2_s, 1024
        if u == GAIN:
            return own_g, outb_g, rx0_g, rx1_g, rx2_g, f2_g, 256
        return own.at[u], outb.at[u % OUT_SLOTS], rx0.at[u], rx1.at[u], rx2.at[u], f2.at[u], 256

    def step0(u):
        _, out_r, r0, _, _, _, _ = bufs(u)
        return pltpu.make_async_remote_copy(
            src_ref=out_r, dst_ref=r0, send_sem=ss0.at[u], recv_sem=rs0.at[u],
            device_id=peer(3, 1), device_id_type=MESH,
        )

    def chunk(ref, rows, which, part, parts):
        size = rows // 4 // parts
        return ref.at[pl.ds(pl.multiple_of(which * (rows // 4) + part * size, size), size)]

    def step1(u):
        o, _, _, r1, _, _, rows = bufs(u)
        axis = ORDER[CLASS[u]][0]
        p = along(axis)
        plan = (
            ((p + 2) % 4, 0, 1), ((p + 1) % 4, 1, 1),
            ((p + 2) % 4, 1, 3), ((p + 3) % 4, 0, 3),
            ((p + 1) % 4, 0, 1), ((p + 3) % 4, 1, 3),
        )
        return [
            pltpu.make_async_remote_copy(
                src_ref=chunk(o, rows, which, part, 2), dst_ref=r1.at[n],
                send_sem=ss1.at[6 * u + n], recv_sem=rs1.at[6 * u + n],
                device_id=peer(axis, way), device_id_type=MESH,
            )
            for n, (which, part, way) in enumerate(plan)
        ]

    def step2(u):
        o, _, _, _, r2, _, rows = bufs(u)
        first, second, _ = ORDER[CLASS[u]]
        p1, p2 = along(first), along(second)
        size = rows // 16
        return [
            pltpu.make_async_remote_copy(
                src_ref=o.at[pl.ds(pl.multiple_of(p1 * (rows // 4) + ((p2 + j) % 4) * size, size), size)],
                dst_ref=r2.at[j - 1],
                send_sem=ss2.at[3 * u + j - 1], recv_sem=rs2.at[3 * u + j - 1],
                device_id=peer(second, j), device_id_type=MESH,
            )
            for j in (1, 2, 3)
        ]

    def step3(n):
        if n < NPAIRS:
            k, src, dst = CLASS[PAIRS[n][0]], s3.at[n], rx3.at[n]
        elif n == NPAIRS:
            k, src, dst = 2, s3_s, rx3_s
        else:
            k, src, dst = 2, s3_g, rx3_g
        axis = ORDER[k][2]
        p = along(axis)
        return [
            pltpu.make_async_remote_copy(
                src_ref=src.at[(p + j) % 4], dst_ref=dst.at[j - 1],
                send_sem=ss3.at[3 * n + j - 1], recv_sem=rs3.at[3 * n + j - 1],
                device_id=peer(axis, j), device_id_type=MESH,
            )
            for j in (1, 2, 3)
        ]

    def start(copies):
        for one in copies:
            one.start()

    done2 = set()

    def service(tick):
        u = tick
        if u < NUNITS:
            start([step0(u)])
        u = tick - D0
        if 0 <= u < NUNITS:
            o, _, r0, _, _, _, rows = bufs(u)
            step0(u).wait_recv()
            o[...] = o[...] + r0[...]
            start(step1(u)[:4])
        u = tick - D1
        if 0 <= u < NUNITS:
            o, _, _, r1, _, _, rows = bufs(u)
            copies = step1(u)
            p = along(ORDER[CLASS[u]][0])
            for first, second, which, part in ((0, 4, (p + 1) % 4, 0), (2, 5, (p + 3) % 4, 1)):
                copies[first].wait_recv()
                view = chunk(o, rows, which, part, 2)
                view[...] = view[...] + r1[first]
                start([copies[second]])
        u = tick - D2
        if 0 <= u < NUNITS:
            o, _, _, r1, _, _, rows = bufs(u)
            copies = step1(u)
            p = along(ORDER[CLASS[u]][0])
            for direct, summed, part in ((3, 4, 0), (1, 5, 1)):
                copies[direct].wait_recv()
                copies[summed].wait_recv()
                view = chunk(o, rows, p, part, 2)
                view[...] = view[...] + r1[direct] + r1[summed]
            start(step2(u))
        u = tick - D3
        if 0 <= u < NUNITS:
            o, _, _, _, r2, ff, rows = bufs(u)
            first, second, _ = ORDER[CLASS[u]]
            for copy in step2(u):
                copy.wait_recv()
            size = rows // 16
            at = pl.multiple_of(along(first) * (rows // 4) + along(second) * size, size)
            value = o[pl.ds(at, size)] + r2[0] + r2[1] + r2[2]
            if u == SEC:
                for n in range(4):
                    s3_s[n] = value[16 * n : 16 * n + 16]
                start(step3(NPAIRS))
            elif u == GAIN:
                for n in range(4):
                    s3_g[n] = jnp.concatenate(
                        [value[4 * n : 4 * n + 4, 0:128], value[4 * n : 4 * n + 4, 128:256]], axis=0
                    )
                start(step3(NPAIRS + 1))
            else:
                ff[...] = value
                done2.add(u)
                for n, (ua, ub) in enumerate(PAIRS):
                    if u in (ua, ub) and ua in done2 and ub in done2:
                        va, vb = f2[ua], f2[ub]
                        for q in range(4):
                            s3[n, q] = jnp.concatenate([va[4 * q : 4 * q + 4], vb[4 * q : 4 * q + 4]], axis=0)
                        start(step3(n))

    def put(u, a, g):
        rows = a.shape[0]
        xt[:, 0:rows] = dot_nt(order_of(CLASS[u]), a).astype(BF16)
        if u >= OUT_SLOTS:
            step0(u - OUT_SLOTS).wait_send()
        o, out_r = bufs(u)[:2]
        value = dot(xt[:, 0:rows], g)
        o[...] = value[0:256]
        out_r[...] = value[256:512]

    tick = 0
    for layer in (1, 0):
        def gates(t, layer=layer):
            scalar = mx[layer, 0:ATOMS, lanes(t)]
            gate = jax.nn.sigmoid(scalar)
            dy0 = dyb[0:ATOMS, lanes(t)]
            dgate = jnp.zeros((ATOMS, 128), F32)
            dskip = dy0 * xb[layer, 0:ATOMS, lanes(t)].astype(F32)
            for m in range(1, 16):
                dy = dyb[comp_rows(m), lanes(t)]
                dmx[comp_rows(m), lanes(t)] = (dy * gate).astype(BF16)
                dgate += dy * mx[layer, comp_rows(m), lanes(t)]
                dskip += dy * xb[layer, comp_rows(m), lanes(t)].astype(F32)
            slope = gate * (1.0 - gate)
            dmx[0:ATOMS, lanes(t)] = (dy0 * (gate + scalar * slope) + dgate * slope).astype(BF16)
            dsk[layer, :, lanes(t)] = dskip

        each_tile(gates)
        if layer == 1:
            pl.semaphore_wait(barrier, 22)
        for d, (a, b) in enumerate(LEVELS):
            put(tick, sm[layer, rows_of(a, b), :], dmx[rows_of(a, b), :])
            service(tick)
            tick += 1
        for d, (a, b) in enumerate(LEVELS):
            dsb[rows_of(a, b), :] = dot_nt(dmx[rows_of(a, b), :], wout[layer, d]) * 0.25

        def back(t, layer=layer):
            for s in range(4):
                src0 = lg[layer, 0, edge_rows(s), lanes(t)].astype(F32)
                total0 = jnp.zeros((ATOMS, 128), F32)
                for d, (a, b) in enumerate(LEVELS):
                    weight = rad[layer, edge_rows(s), lanes(t, d * C)]
                    by_harm = jnp.zeros((ATOMS, 128), F32)
                    by_src = jnp.zeros((ATOMS, 128), F32)
                    for m in range(a, b):
                        dt = dsb[comp_rows(m), lanes(t)]
                        by_harm += abc[m, edge_rows(s), :] * dt
                        if m == 0:
                            by_src += dt * src0
                            total0 += dt * weight
                        else:
                            by_src += dt * lg[layer, m, edge_rows(s), lanes(t)].astype(F32)
                            lg[layer, m, edge_rows(s), lanes(t)] = (dt * weight).astype(BF16)
                    dr[layer, edge_rows(s), lanes(t, d * C)] = (by_harm * src0 + by_src).astype(BF16)
                    total0 += weight * by_harm
                lg[layer, 0, edge_rows(s), lanes(t)] = total0.astype(BF16)

        each_tile(back)
        for m in range(16):
            dl[comp_rows(m), :] = dot(scatter, lg[layer, m]).astype(BF16)

        for d, (a, b) in enumerate(LEVELS):
            put(tick, xb[layer, rows_of(a, b), :], dl[rows_of(a, b), :])
            service(tick)
            tick += 1
        for d, (a, b) in enumerate(LEVELS):
            dsb[rows_of(a, b), :] = dot_nt(dl[rows_of(a, b), :], wup[layer, d])

        def skip(t, layer=layer):
            skip_gain = grow[layer, :, lanes(t)]
            for m in range(16):
                dyb[comp_rows(m), lanes(t)] = (
                    dsb[comp_rows(m), lanes(t)] + skip_gain * dyb[comp_rows(m), lanes(t)]
                )

        each_tile(skip)

    first_term = jnp.zeros((8, 128), F32)
    for layer in (0, 1):
        for d in range(4):
            drt[layer, d] = dot_nt(order_of(3), dr[layer, :, d * C : (d + 1) * C]).astype(BF16)
        dhid = dot_nt(dr[layer], wsec[layer])
        p = pre[layer]
        sg = jax.nn.sigmoid(p)
        dpre = dhid * (sg * (1.0 + p * (1.0 - sg)))
        first_term += dot(basis2, dpre, HIGH)
    red[0, 0:8] = first_term
    for d in range(4):
        blk = dot(drt[0, d], hid[0]) + dot(drt[1, d], hid[1])
        own_s[256 * d : 256 * d + 256, :] = blk[0:256]
        outb_s[256 * d : 256 * d + 256, :] = blk[256:512]
    service(tick)
    tick += 1
    for layer in (0, 1):
        hi = dsk[layer].astype(BF16)
        lo = (dsk[layer] - hi.astype(F32)).astype(BF16)
        blk = dot(dot_nt(order_of(2), hi).astype(BF16), kind_b) + dot(dot_nt(order_of(2), lo).astype(BF16), kind_b)
        own_g[:, 128 * layer : 128 * layer + 128] = blk[0:256]
        outb_g[:, 128 * layer : 128 * layer + 128] = blk[256:512]
    service(tick)
    tick += 1

    fgb[...] = dot(picks((r & 15) * 32 + (r >> 4)), dyb[...].astype(BF16)).astype(BF16)
    save = pltpu.make_async_copy(fgb, fg_o, wsem.at[6])
    save.start()

    def all_sum(stage, n):
        p = lax.axis_index("inner") if stage == 0 else lax.axis_index("outer")
        base = 8 * stage

        def copy(j, slot):
            return pltpu.make_async_remote_copy(
                src_ref=red.at[stage], dst_ref=redrx.at[base + slot],
                send_sem=ssr.at[base + j], recv_sem=rsr.at[base + slot],
                device_id=group_peer(stage, j), device_id_type=MESH,
            )

        return [copy(j, p) for j in range(1, n)], [copy(j, (p + j) % n) for j in range(1, n)], base, p

    while tick < NUNITS + D3:
        service(tick)
        tick += 1

    squares = jnp.zeros((8, 128), F32)
    for n in range(NPAIRS + 2):
        if n < NPAIRS:
            src, rec, out, k = s3.at[n], rx3.at[n], fin.at[n], CLASS[PAIRS[n][0]]
        elif n == NPAIRS:
            src, rec, out, k = s3_s, rx3_s, fin_s, 2
        else:
            src, rec, out, k = s3_g, rx3_g, fin_g, 2
        for copy in step3(n):
            copy.wait_recv()
        value = src[along(ORDER[k][2])] + rec[0] + rec[1] + rec[2]
        out[...] = value
        sq = value * value
        if n < NPAIRS:
            for q in range(4):
                squares += sq[:, 128 * q : 128 * q + 128]
        elif n == NPAIRS:
            squares += sq[0:8] + sq[8:16]
        else:
            squares += sq
    red[0, 8:16] = squares
    for stage, n in GROUPS:
        copies, waits, base, p = all_sum(stage, n)
        for one in copies:
            one.start()
        redrx[base + p] = red[stage]
        if stage == 0:
            for u in range(NUNITS):
                if not (u < 16 and u + OUT_SLOTS < 16):
                    step0(u).wait_send()
                for copy in step1(u) + step2(u):
                    copy.wait_send()
            for q in range(NPAIRS + 2):
                for copy in step3(q):
                    copy.wait_send()
        for one in waits:
            one.wait_recv()
        value = redrx[base]
        for j in range(1, n):
            value = value + redrx[base + j]
        red[stage + 1] = value
    sums[...] = red[2]

    for stage, n in GROUPS:
        for copy in all_sum(stage, n)[0]:
            copy.wait_send()
    save.wait()


def finish(fin, fin_s, fin_g, sums, fg, up_o, first_o, sec_o, out_o, gain_o, fg_o):
    fg_o[...] = fg[...]
    first_sum = sums[0:8]
    total = sums[8:16] + first_sum * first_sum
    total = jnp.sum(jnp.sum(total, axis=1, keepdims=True), axis=0, keepdims=True)
    scale = jnp.minimum(1.0, CLIP_NORM / jnp.sqrt(total + 1e-6))
    for n, pair in enumerate(PAIRS):
        value = fin[n] * scale
        for half, u in enumerate(pair):
            which, layer, d = MATS[u]
            ref = up_o if which == "up" else out_o
            ref[layer, d] = value[4 * half : 4 * half + 4]
    scaled = first_sum * scale
    second = fin_s[...] * scale
    gains = fin_g[...] * scale
    for layer in (0, 1):
        first_o[layer] = scaled[:, 64 * layer : 64 * layer + 64]
        sec_o[layer] = second[:, 64 * layer : 64 * layer + 64]
        gain_o[layer] = gains[4 * layer : 4 * layer + 4, 0:89]


def per_device(features, cotangent, counts, senders, angular, basis, species, w_up, w_first, w_second, w_out, gain):
    vm, hbm = pl.BlockSpec(memory_space=pltpu.VMEM), pl.BlockSpec(memory_space=pl.ANY)
    V = pltpu.VMEM
    dma = pltpu.SemaphoreType.DMA
    scratch = [
        V((C, C), BF16), V((C, C), BF16), V((89, 2, C), F32),
        V((2, 4, C, C), BF16), V((2, 4, C, C), BF16), V((2, 128, 2048), BF16), V((2, 8, 128), F32), V((2, 128, C), F32), dma((10,)),
        V((2, C, C), BF16),
        V((2, 16, EDGES, C), BF16),
        V((2, EDGES, 2048), F32),
        V((2, EDGES, 128), F32),
        V((2, EDGES, 128), BF16),
        V((2, C, C), BF16),
        V((2, C, C), F32),
        V((2, ATOMS, C), F32),
        V((16, EDGES, 128), F32),
        V((C, C), BF16),
        V((C, C), F32),
        V((C, C), BF16),
        V((C, C), F32),
        V((2, EDGES, 2048), BF16),
        V((C, C), BF16),
        V((2, 4, C, EDGES), BF16),
        V((C, 256), BF16),
        V((4, C, C), BF16),
        V((2, ATOMS, C), F32),
        V((C, C), BF16),
        V((16, 256, C), F32), V((1024, 128), F32), V((256, 256), F32),
        V((OUT_SLOTS, 256, C), F32), V((1024, 128), F32), V((256, 256), F32),
        V((16, 256, C), F32), V((1024, 128), F32), V((256, 256), F32),
        V((16, 6, 32, C), F32), V((6, 128, 128), F32), V((6, 32, 256), F32),
        V((16, 3, 16, C), F32), V((3, 64, 128), F32), V((3, 16, 256), F32),
        V((16, 16, C), F32), V((64, 128), F32), V((16, 256), F32),
        V((NPAIRS, 4, 8, C), F32), V((4, 16, 128), F32), V((4, 8, 128), F32),
        V((NPAIRS, 3, 8, C), F32), V((3, 16, 128), F32), V((3, 8, 128), F32),
        V((3, 16, 128), F32), V((24, 16, 128), F32),
        dma((NUNITS,)), dma((NUNITS,)), dma((6 * NUNITS,)), dma((6 * NUNITS,)),
        dma((3 * NUNITS,)), dma((3 * NUNITS,)), dma((3 * (NPAIRS + 2),)), dma((3 * (NPAIRS + 2),)),
        dma((24,)), dma((24,)),
    ]
    shape = jax.ShapeDtypeStruct
    sums = pl.pallas_call(
        kernel,
        name="interaction_grads",
        out_shape=(
            shape((NPAIRS, 8, C), F32), shape((16, 128), F32), shape((8, 128), F32), shape((16, 128), F32),
            shape((C, C), BF16),
        ),
        in_specs=[pl.BlockSpec(memory_space=pltpu.SMEM)] + [vm] * 5 + [hbm] * 6,
        out_specs=(vm,) * 4 + (hbm,),
        scratch_shapes=scratch,
        compiler_params=pltpu.CompilerParams(
            collective_id=0, has_side_effects=True, vmem_limit_bytes=63 * 2**20
        ),
        cost_estimate=pl.CostEstimate(flops=8 * 10**9, bytes_accessed=12 * 10**6, transcendentals=10**5),
    )(
        counts, senders, angular, basis, species.reshape(1, ATOMS), w_first,
        features.reshape(C, C), cotangent.reshape(C, C), jnp.transpose(gain, (1, 0, 2)), w_up, w_second, w_out,
    )
    up, first, second, out, gain_grad, feature_grad = pl.pallas_call(
        finish,
        name="clip",
        out_shape=(
            shape((2, 4, 4, C), F32), shape((2, 8, 64), F32), shape((2, 16, 64), F32),
            shape((2, 4, 4, C), F32), shape((2, 4, 89), F32), shape((C, C), BF16),
        ),
        in_specs=[vm] * 5,
        out_specs=(vm,) * 6,
    )(*sums)
    return (
        up, first, jnp.transpose(second, (0, 2, 1)), out, jnp.transpose(gain_grad, (0, 2, 1)),
        feature_grad.reshape(features.shape),
    )


def solution(mesh):
    both = ("inner", "outer")
    return jax.shard_map(
        per_device,
        mesh=mesh,
        in_specs=(
            P(both, None, None), P(both, None, None), P(both), P(None, both), P(None, None, both),
            P(None, None, both), P(both), P(), P(), P(), P(), P(),
        ),
        out_specs=(
            P(None, None, both, None), P(), P(None, None, both), P(None, None, both, None),
            P(None, None, both), P(both, None, None),
        ),
        check_vma=False,
    )
```

time: 114 us -> 85.6 us (0.75)
  Pallas kernels: 102 us -> 84.1 us
  local copies, waits for them, and re-layouts: 11 us -> 0 us
    pallas_call x1 -> x2, Pallas kernels: 102 us -> 84.1 us  [the longest x1 82 us: per_device(): pl.pallas_call(kernel, name='interaction_grads', out_shape=(shape((NPAIRS...]
    unnamed x7 -> x0, local copies, waits for them, and re-layouts: 11 us -> none
where the time goes in v2:
time: 85.6 us; the launch traced here: 85.4 us
  Pallas kernels  84.1 us (98%)
  between operations  1.29 us (2%)
    pallas_call x1, Pallas kernels, per_device(): pl.pallas_call(kernel, name='interaction_grads', out_shape=(shape((NPAIRS...  82 us
    pallas_call x1, Pallas kernels, per_device(): pl.pallas_call(finish, name='clip', out_shape=(shape((2, 4, 4, C), F32),...  2.1 us

profile of v2, /device:TPU:1, one launch (start us, length us, event | category | flops | bytes accessed | tf_op | source)
XLA Modules:
  0.0 85.4 jit_solution(15475923193277020570)
XLA Ops:
  1.3 82.0 %interaction_grads.1 = (f32[8,8,512]{2,1,0:T(8,128)}, f32[16,128]{1,0:T(8,128)}, f32[8,128]{1,0:T(8,128)}, f32[16,128]{1,0:T(8,128)}, bf16[512,512]{1,0:T(8,128)(2,1)}) custom-call(s32[1]{0:T(128)S(6)} %copy.18.counts, s32[4,32]{1,0:T(4,128)} %send.1, f32[16,4,32]{2,1,0:T(4,128)} %ang.1, f32[8,4,32]{2,1,0:T(4,128)} %basis.1, s32[1,32]{1,0:T(1,128)} %bitcast.13, ...), custom_call_target="tpu_custom_call" | custom-call | flops 8000000000 | bytes 12000000 | tf_op jit(solution)/shard_map/interaction_grads/pallas_call | solution.py:607
  83.3 2.1 %clip.1 = (f32[2,4,4,512]{3,2,1,0:T(4,128)}, f32[2,8,64]{2,1,0:T(8,128)}, f32[2,16,64]{2,1,0:T(8,128)}, f32[2,4,4,512]{3,2,1,0:T(4,128)}, f32[2,4,89]{2,1,0:T(4,128)}, /*index=5*/bf16[512,512]{1,0:T(8,128)(2,1)}) custom-call(f32[8,8,512]{2,1,0:T(8,128)} %get-tuple-element.17.fin, f32[16,128]{1,0:T(8,128)} %get-tuple-element.18.fin_s, ...), custom_call_target="tpu_custom_call" | custom-call | tf_op jit(solution)/shard_map/clip/pallas_call | solution.py:625

commit v3 on v2

--- a/solution.py
+++ b/solution.py
@@ -34,7 +34,15 @@
     _own = [q for q in range(16) if CLASS[q] == _k]
     PAIRS += [(_own[n], _own[n + 1]) for n in range(0, len(_own), 2)]
 NPAIRS = len(PAIRS)
-D0, D1, D2, D3 = 2, 6, 10, 13
+STEPS = (
+    "G1", "P0", "P1", "P2", "P3", "S1", "K4", "A0", "K5", "K6", "K7", "A1", "L1", "P4", "A2", "P5", "A3", "P6", "P7",
+    "B0", "X1", "B1", "A4", "G0", "A5", "P8", "B2", "A6", "P9", "B3", "P10", "A7", "P11", "A8", "S0", "C1", "K0",
+    "A9", "B5", "K1", "K2", "K3", "B4", "A10", "C0", "P16", "A11", "L0", "B6", "P12", "P13", "C2", "P14", "B7",
+    "A16", "P15", "B8", "P17", "A12", "C3", "X0", "A13", "R0", "A14", "C4", "F0", "A15", "C5", "A17", "D1", "B10",
+    "B9", "D0", "B11", "C6", "D2", "C7", "B12", "B16", "B13", "C8", "D4", "B14", "B15", "D3", "B17", "C9", "D5",
+    "C11", "C10", "D7", "D6", "C13", "C12", "C16", "C15", "E3", "D8", "C17", "C14", "E6", "D9", "E0", "D10", "D12",
+    "D11", "D13", "D15", "D16", "D14", "E4", "D17", "E1", "E7", "E8", "E2", "E5", "E9",
+)
 OUT_SLOTS = 4
 
 
@@ -51,6 +59,10 @@
 
 
 GROUPS = ((0, 8), (1, 16))
+
+
+def dot_tn(a, b):
+    return lax.dot_general(a, b, (((0,), (0,)), ((), ())), preferred_element_type=F32)
 
 
 def position():
@@ -99,7 +111,7 @@
     counts, send, ang, basis, spec, w_first, feat_h, cot_h, gain_h, wup_h, wsec_h, wout_h,
     fin, fin_s, fin_g, sums, fg_o,
     feat, cot, gain, wup, wout, wsec, wfp, gpad, wsem,
-    xb, lg, rad, pre, hid, sm, mx, grow, abc, lbuf, dyb, dmx, dsb, dr, dl, drt, xt, pt, dsk, fgb,
+    xb, lg, rad, pre, hid, sm, mx, grow, abc, lbuf, dyb, dmx, dsb, dr, dl, turn, xt, pt, dsk, fgb,
     own, own_s, own_g, outb, outb_s, outb_g,
     rx0, rx0_s, rx0_g, rx1, rx1_s, rx1_g, rx2, rx2_s, rx2_g,
     f2, f2_s, f2_g, s3, s3_s, s3_g, rx3, rx3_s, rx3_g,
@@ -117,7 +129,7 @@
         loads["out", layer] = pltpu.make_async_copy(wout_h.at[layer], wout.at[layer], wsem.at[3 * layer + 2])
     for n, (name, src, dst) in enumerate((("feat", feat_h, feat), ("gain", gain_h, gain), ("cot", cot_h, cot))):
         loads[name] = pltpu.make_async_copy(src, dst, wsem.at[7 + n])
-    for name in ("feat", ("up", 0), ("sec", 0), "gain", ("out", 0), ("up", 1), ("sec", 1), ("out", 1), "cot"):
+    for name in ("feat", ("up", 0), ("sec", 0)):
         loads[name].start()
 
     barrier = pltpu.get_barrier_semaphore()
@@ -142,12 +154,9 @@
     def order_of(k):
         if k not in made:
             made.add(k)
-            if k == 3:
-                pt[k] = picks(r ^ (c << 8))
-            else:
-                digits = ((r >> 6) & 3, (r >> 4) & 3, (r >> 2) & 3)
-                held = {ORDER[k][n]: digits[n] for n in range(3)}
-                pt[k] = picks(held[0] * 128 + ((r >> 8) ^ c) * 64 + held[1] * 16 + held[2] * 4 + (r & 3))
+            digits = ((r >> 6) & 3, (r >> 4) & 3, (r >> 2) & 3)
+            held = {ORDER[k][n]: digits[n] for n in range(3)}
+            pt[k] = picks(held[0] * 128 + ((r >> 8) ^ c) * 64 + held[1] * 16 + held[2] * 4 + (r & 3))
         return pt[k]
 
     eye_e = onehot(iota((EDGES, EDGES), 0) == iota((EDGES, EDGES), 1))
@@ -172,6 +181,8 @@
         return pl.ds(m * ATOMS, ATOMS)
 
     def lanes(t, base=0):
+        if isinstance(t, int):
+            return pl.ds(base + t * 128, 128)
         return pl.ds(pl.multiple_of(base + t * 128, 128), 128)
 
     def each_tile(body):
@@ -189,6 +200,9 @@
         for d in range(4):
             rad[layer, :, d * C : (d + 1) * C] = dot(hid[layer], wsec[layer, :, d * C : (d + 1) * C])
         loads["up", layer].wait()
+        if layer == 0:
+            for name in (("out", 0), "gain", ("up", 1), ("sec", 1)):
+                loads[name].start()
         for d, (a, b) in enumerate(LEVELS):
             lbuf[rows_of(a, b), :] = dot(xb[layer, rows_of(a, b), :], wup[layer, d]).astype(BF16)
         for m in range(16):
@@ -208,6 +222,9 @@
 
         each_tile(message)
         loads["out", layer].wait()
+        if layer == 0:
+            for name in ("cot", ("out", 1)):
+                loads[name].start()
         for d, (a, b) in enumerate(LEVELS):
             mx[layer, rows_of(a, b), :] = dot(sm[layer, rows_of(a, b), :], wout[layer, d])
         if layer == 0:
@@ -309,65 +326,80 @@
 
     done2 = set()
 
-    def service(tick):
-        u = tick
-        if u < NUNITS:
-            start([step0(u)])
-        u = tick - D0
-        if 0 <= u < NUNITS:
-            o, _, r0, _, _, _, rows = bufs(u)
-            step0(u).wait_recv()
-            o[...] = o[...] + r0[...]
-            start(step1(u)[:4])
-        u = tick - D1
-        if 0 <= u < NUNITS:
-            o, _, _, r1, _, _, rows = bufs(u)
-            copies = step1(u)
-            p = along(ORDER[CLASS[u]][0])
-            for first, second, which, part in ((0, 4, (p + 1) % 4, 0), (2, 5, (p + 3) % 4, 1)):
-                copies[first].wait_recv()
-                view = chunk(o, rows, which, part, 2)
-                view[...] = view[...] + r1[first]
-                start([copies[second]])
-        u = tick - D2
-        if 0 <= u < NUNITS:
-            o, _, _, r1, _, _, rows = bufs(u)
-            copies = step1(u)
-            p = along(ORDER[CLASS[u]][0])
-            for direct, summed, part in ((3, 4, 0), (1, 5, 1)):
-                copies[direct].wait_recv()
-                copies[summed].wait_recv()
-                view = chunk(o, rows, p, part, 2)
-                view[...] = view[...] + r1[direct] + r1[summed]
-            start(step2(u))
-        u = tick - D3
-        if 0 <= u < NUNITS:
-            o, _, _, _, r2, ff, rows = bufs(u)
-            first, second, _ = ORDER[CLASS[u]]
-            for copy in step2(u):
-                copy.wait_recv()
-            size = rows // 16
-            at = pl.multiple_of(along(first) * (rows // 4) + along(second) * size, size)
-            value = o[pl.ds(at, size)] + r2[0] + r2[1] + r2[2]
-            if u == SEC:
-                for n in range(4):
-                    s3_s[n] = value[16 * n : 16 * n + 16]
-                start(step3(NPAIRS))
-            elif u == GAIN:
-                for n in range(4):
-                    s3_g[n] = jnp.concatenate(
-                        [value[4 * n : 4 * n + 4, 0:128], value[4 * n : 4 * n + 4, 128:256]], axis=0
-                    )
-                start(step3(NPAIRS + 1))
-            else:
-                ff[...] = value
-                done2.add(u)
-                for n, (ua, ub) in enumerate(PAIRS):
-                    if u in (ua, ub) and ua in done2 and ub in done2:
-                        va, vb = f2[ua], f2[ub]
-                        for q in range(4):
-                            s3[n, q] = jnp.concatenate([va[4 * q : 4 * q + 4], vb[4 * q : 4 * q + 4]], axis=0)
-                        start(step3(n))
+    def from_core(u):
+        o, _, r0, _, _, _, _ = bufs(u)
+        step0(u).wait_recv()
+        o[...] = o[...] + r0[...]
+        start(step1(u)[:4])
+
+    def pass_on(u):
+        o, _, _, r1, _, _, rows = bufs(u)
+        copies = step1(u)
+        p = along(ORDER[CLASS[u]][0])
+        for first, second, which, part in ((0, 4, (p + 1) % 4, 0), (2, 5, (p + 3) % 4, 1)):
+            copies[first].wait_recv()
+            view = chunk(o, rows, which, part, 2)
+            view[...] = view[...] + r1[first]
+            start([copies[second]])
+
+    def end_first(u):
+        o, _, _, r1, _, _, rows = bufs(u)
+        copies = step1(u)
+        p = along(ORDER[CLASS[u]][0])
+        for direct, summed, part in ((3, 4, 0), (1, 5, 1)):
+            copies[direct].wait_recv()
+            copies[summed].wait_recv()
+            view = chunk(o, rows, p, part, 2)
+            view[...] = view[...] + r1[direct] + r1[summed]
+        start(step2(u))
+
+    def end_second(u):
+        o, _, _, _, r2, ff, rows = bufs(u)
+        first, second, _ = ORDER[CLASS[u]]
+        for copy in step2(u):
+            copy.wait_recv()
+        size = rows // 16
+        at = pl.multiple_of(along(first) * (rows // 4) + along(second) * size, size)
+        value = o[pl.ds(at, size)] + r2[0] + r2[1] + r2[2]
+        if u == SEC:
+            for n in range(4):
+                s3_s[n] = value[16 * n : 16 * n + 16]
+            start(step3(NPAIRS))
+        elif u == GAIN:
+            for n in range(4):
+                s3_g[n] = jnp.concatenate(
+                    [value[4 * n : 4 * n + 4, 0:128], value[4 * n : 4 * n + 4, 128:256]], axis=0
+                )
+            start(step3(NPAIRS + 1))
+        else:
+            ff[...] = value
+            done2.add(u)
+            for n, (ua, ub) in enumerate(PAIRS):
+                if u in (ua, ub) and ua in done2 and ub in done2:
+                    va, vb = f2[ua], f2[ub]
+                    for q in range(4):
+                        s3[n, q] = jnp.concatenate([va[4 * q : 4 * q + 4], vb[4 * q : 4 * q + 4]], axis=0)
+                    start(step3(n))
+
+    red[0] = jnp.zeros((16, 128), F32)
+
+    def end_third(n):
+        if n < NPAIRS:
+            src, rec, out, k = s3.at[n], rx3.at[n], fin.at[n], CLASS[PAIRS[n][0]]
+        elif n == NPAIRS:
+            src, rec, out, k = s3_s, rx3_s, fin_s, 2
+        else:
+            src, rec, out, k = s3_g, rx3_g, fin_g, 2
+        for copy in step3(n):
+            copy.wait_recv()
+        value = src[along(ORDER[k][2])] + rec[0] + rec[1] + rec[2]
+        out[...] = value
+        sq = value * value
+        if n < NPAIRS:
+            sq = sq[:, 0:128] + sq[:, 128:256] + sq[:, 256:384] + sq[:, 384:512]
+        elif n == NPAIRS:
+            sq = sq[0:8] + sq[8:16]
+        red[0, 8:16] = red[0, 8:16] + sq
 
     def put(u, a, g):
         rows = a.shape[0]
@@ -378,10 +410,10 @@
         value = dot(xt[:, 0:rows], g)
         o[...] = value[0:256]
         out_r[...] = value[256:512]
-
-    tick = 0
-    for layer in (1, 0):
-        def gates(t, layer=layer):
+        start([step0(u)])
+
+    def gates(layer):
+        def tile(t):
             scalar = mx[layer, 0:ATOMS, lanes(t)]
             gate = jax.nn.sigmoid(scalar)
             dy0 = dyb[0:ATOMS, lanes(t)]
@@ -396,85 +428,108 @@
             dmx[0:ATOMS, lanes(t)] = (dy0 * (gate + scalar * slope) + dgate * slope).astype(BF16)
             dsk[layer, :, lanes(t)] = dskip
 
-        each_tile(gates)
+        each_tile(tile)
         if layer == 1:
             pl.semaphore_wait(barrier, 22)
-        for d, (a, b) in enumerate(LEVELS):
-            put(tick, sm[layer, rows_of(a, b), :], dmx[rows_of(a, b), :])
-            service(tick)
-            tick += 1
+
+    def product(u):
+        if u == SEC:
+            second_product()
+        elif u == GAIN:
+            gain_product()
+        else:
+            which, layer, d = MATS[u]
+            rows = rows_of(*LEVELS[d])
+            if which == "out":
+                put(u, sm[layer, rows, :], dmx[rows, :])
+            else:
+                put(u, xb[layer, rows, :], dl[rows, :])
+
+    def summed_grad(layer):
         for d, (a, b) in enumerate(LEVELS):
             dsb[rows_of(a, b), :] = dot_nt(dmx[rows_of(a, b), :], wout[layer, d]) * 0.25
 
-        def back(t, layer=layer):
-            for s in range(4):
-                src0 = lg[layer, 0, edge_rows(s), lanes(t)].astype(F32)
-                total0 = jnp.zeros((ATOMS, 128), F32)
-                for d, (a, b) in enumerate(LEVELS):
-                    weight = rad[layer, edge_rows(s), lanes(t, d * C)]
-                    by_harm = jnp.zeros((ATOMS, 128), F32)
-                    by_src = jnp.zeros((ATOMS, 128), F32)
-                    for m in range(a, b):
-                        dt = dsb[comp_rows(m), lanes(t)]
-                        by_harm += abc[m, edge_rows(s), :] * dt
-                        if m == 0:
-                            by_src += dt * src0
-                            total0 += dt * weight
-                        else:
-                            by_src += dt * lg[layer, m, edge_rows(s), lanes(t)].astype(F32)
-                            lg[layer, m, edge_rows(s), lanes(t)] = (dt * weight).astype(BF16)
-                    dr[layer, edge_rows(s), lanes(t, d * C)] = (by_harm * src0 + by_src).astype(BF16)
-                    total0 += weight * by_harm
-                lg[layer, 0, edge_rows(s), lanes(t)] = total0.astype(BF16)
-
-        each_tile(back)
+    def message_grad(n):
+        layer, t = n // 4, n % 4
+        for s in range(4):
+            src0 = lg[layer, 0, edge_rows(s), lanes(t)].astype(F32)
+            total0 = jnp.zeros((ATOMS, 128), F32)
+            for d, (a, b) in enumerate(LEVELS):
+                weight = rad[layer, edge_rows(s), lanes(t, d * C)]
+                by_harm = jnp.zeros((ATOMS, 128), F32)
+                by_src = jnp.zeros((ATOMS, 128), F32)
+                for m in range(a, b):
+                    dt = dsb[comp_rows(m), lanes(t)]
+                    by_harm += abc[m, edge_rows(s), :] * dt
+                    if m == 0:
+                        by_src += dt * src0
+                        total0 += dt * weight
+                    else:
+                        by_src += dt * lg[layer, m, edge_rows(s), lanes(t)].astype(F32)
+                        lg[layer, m, edge_rows(s), lanes(t)] = (dt * weight).astype(BF16)
+                dr[layer, edge_rows(s), lanes(t, d * C)] = (by_harm * src0 + by_src).astype(BF16)
+                total0 += weight * by_harm
+            lg[layer, 0, edge_rows(s), lanes(t)] = total0.astype(BF16)
+
+    def lifted_grad(layer):
         for m in range(16):
             dl[comp_rows(m), :] = dot(scatter, lg[layer, m]).astype(BF16)
 
-        for d, (a, b) in enumerate(LEVELS):
-            put(tick, xb[layer, rows_of(a, b), :], dl[rows_of(a, b), :])
-            service(tick)
-            tick += 1
+    def input_grad(layer):
         for d, (a, b) in enumerate(LEVELS):
             dsb[rows_of(a, b), :] = dot_nt(dl[rows_of(a, b), :], wup[layer, d])
 
-        def skip(t, layer=layer):
+        def tile(t):
             skip_gain = grow[layer, :, lanes(t)]
             for m in range(16):
                 dyb[comp_rows(m), lanes(t)] = (
                     dsb[comp_rows(m), lanes(t)] + skip_gain * dyb[comp_rows(m), lanes(t)]
                 )
 
-        each_tile(skip)
-
-    first_term = jnp.zeros((8, 128), F32)
-    for layer in (0, 1):
+        each_tile(tile)
+
+    def radial_grad(_):
+        term = jnp.zeros((8, 128), F32)
+        for layer in (0, 1):
+            dhid = dot_nt(dr[layer], wsec[layer])
+            p = pre[layer]
+            sg = jax.nn.sigmoid(p)
+            term += dot(basis2, dhid * (sg * (1.0 + p * (1.0 - sg))), HIGH)
+        red[0, 0:8] = term
+
+    def second_product():
         for d in range(4):
-            drt[layer, d] = dot_nt(order_of(3), dr[layer, :, d * C : (d + 1) * C]).astype(BF16)
-        dhid = dot_nt(dr[layer], wsec[layer])
-        p = pre[layer]
-        sg = jax.nn.sigmoid(p)
-        dpre = dhid * (sg * (1.0 + p * (1.0 - sg)))
-        first_term += dot(basis2, dpre, HIGH)
-    red[0, 0:8] = first_term
-    for d in range(4):
-        blk = dot(drt[0, d], hid[0]) + dot(drt[1, d], hid[1])
-        own_s[256 * d : 256 * d + 256, :] = blk[0:256]
-        outb_s[256 * d : 256 * d + 256, :] = blk[256:512]
-    service(tick)
-    tick += 1
-    for layer in (0, 1):
-        hi = dsk[layer].astype(BF16)
-        lo = (dsk[layer] - hi.astype(F32)).astype(BF16)
-        blk = dot(dot_nt(order_of(2), hi).astype(BF16), kind_b) + dot(dot_nt(order_of(2), lo).astype(BF16), kind_b)
-        own_g[:, 128 * layer : 128 * layer + 128] = blk[0:256]
-        outb_g[:, 128 * layer : 128 * layer + 128] = blk[256:512]
-    service(tick)
-    tick += 1
-
-    fgb[...] = dot(picks((r & 15) * 32 + (r >> 4)), dyb[...].astype(BF16)).astype(BF16)
-    save = pltpu.make_async_copy(fgb, fg_o, wsem.at[6])
-    save.start()
+            wide = slice(d * C, (d + 1) * C)
+            blk = dot_tn(hid[0], dr[0, :, wide]) + dot_tn(hid[1], dr[1, :, wide])
+            turn[...] = jnp.transpose(blk)
+            own_s[256 * d : 256 * d + 256, :] = turn[pl.ds(pl.multiple_of(c * 256, 256), 256), :]
+            outb_s[256 * d : 256 * d + 256, :] = turn[pl.ds(pl.multiple_of((1 - c) * 256, 256), 256), :]
+        start([step0(SEC)])
+
+    def gain_product():
+        for layer in (0, 1):
+            hi = dsk[layer].astype(BF16)
+            lo = (dsk[layer] - hi.astype(F32)).astype(BF16)
+            rows = dot_nt(order_of(2), jnp.concatenate([hi, lo], axis=0)).astype(BF16)
+            blk = dot(rows, jnp.concatenate([kind_b, kind_b], axis=0))
+            own_g[:, 128 * layer : 128 * layer + 128] = blk[0:256]
+            outb_g[:, 128 * layer : 128 * layer + 128] = blk[256:512]
+        start([step0(GAIN)])
+
+    saves = []
+
+    def feature_grad(_):
+        fgb[...] = dot(picks((r & 15) * 32 + (r >> 4)), dyb[...].astype(BF16)).astype(BF16)
+        saves.append(pltpu.make_async_copy(fgb, fg_o, wsem.at[6]))
+        saves[0].start()
+
+    actions = {
+        "G": gates, "P": product, "S": summed_grad, "K": message_grad, "L": lifted_grad, "X": input_grad,
+        "R": radial_grad, "F": feature_grad,
+        "A": from_core, "B": pass_on, "C": end_first, "D": end_second, "E": end_third,
+    }
+    for step in STEPS:
+        actions[step[0]](int(step[1:]))
 
     def all_sum(stage, n):
         p = lax.axis_index("inner") if stage == 0 else lax.axis_index("outer")
@@ -489,31 +544,6 @@
 
         return [copy(j, p) for j in range(1, n)], [copy(j, (p + j) % n) for j in range(1, n)], base, p
 
-    while tick < NUNITS + D3:
-        service(tick)
-        tick += 1
-
-    squares = jnp.zeros((8, 128), F32)
-    for n in range(NPAIRS + 2):
-        if n < NPAIRS:
-            src, rec, out, k = s3.at[n], rx3.at[n], fin.at[n], CLASS[PAIRS[n][0]]
-        elif n == NPAIRS:
-            src, rec, out, k = s3_s, rx3_s, fin_s, 2
-        else:
-            src, rec, out, k = s3_g, rx3_g, fin_g, 2
-        for copy in step3(n):
-            copy.wait_recv()
-        value = src[along(ORDER[k][2])] + rec[0] + rec[1] + rec[2]
-        out[...] = value
-        sq = value * value
-        if n < NPAIRS:
-            for q in range(4):
-                squares += sq[:, 128 * q : 128 * q + 128]
-        elif n == NPAIRS:
-            squares += sq[0:8] + sq[8:16]
-        else:
-            squares += sq
-    red[0, 8:16] = squares
     for stage, n in GROUPS:
         copies, waits, base, p = all_sum(stage, n)
         for one in copies:
@@ -539,7 +569,7 @@
     for stage, n in GROUPS:
         for copy in all_sum(stage, n)[0]:
             copy.wait_send()
-    save.wait()
+    saves[0].wait()
 
 
 def finish(fin, fin_s, fin_g, sums, fg, up_o, first_o, sec_o, out_o, gain_o, fg_o):
@@ -585,9 +615,9 @@
         V((C, C), F32),
         V((2, EDGES, 2048), BF16),
         V((C, C), BF16),
-        V((2, 4, C, EDGES), BF16),
+        V((C, 128), F32),
         V((C, 256), BF16),
-        V((4, C, C), BF16),
+        V((3, C, C), BF16),
         V((2, ATOMS, C), F32),
         V((C, C), BF16),
         V((16, 256, C), F32), V((1024, 128), F32), V((256, 256), F32),

time: 85.6 us -> 79.8 us (0.932)
  Pallas kernels: 84.1 us -> 78.3 us
    pallas_call x1, Pallas kernels: 82 us -> 76.2 us  [per_device(): pl.pallas_call(kernel, name='interaction_grads', out_shape=(shape((NPAIRS...]
where the time goes in v3:
time: 79.8 us; the launch traced here: 79.6 us
  Pallas kernels  78.3 us (98%)
  between operations  1.29 us (2%)
    pallas_call x1, Pallas kernels, per_device(): pl.pallas_call(kernel, name='interaction_grads', out_shape=(shape((NPAIRS...  76.2 us
    pallas_call x1, Pallas kernels, per_device(): pl.pallas_call(finish, name='clip', out_shape=(shape((2, 4, 4, C), F32),...  2.1 us

profile of v3, /device:TPU:1, one launch (start us, length us, event | category | flops | bytes accessed | tf_op | source)
XLA Modules:
  0.0 79.6 jit_solution(13441221286991445425)
XLA Ops:
  1.3 76.2 %interaction_grads.1 = (f32[8,8,512]{2,1,0:T(8,128)}, f32[16,128]{1,0:T(8,128)}, f32[8,128]{1,0:T(8,128)}, f32[16,128]{1,0:T(8,128)}, bf16[512,512]{1,0:T(8,128)(2,1)}) custom-call(s32[1]{0:T(128)S(6)} %copy.18.counts, s32[4,32]{1,0:T(4,128)} %send.1, f32[16,4,32]{2,1,0:T(4,128)} %ang.1, f32[8,4,32]{2,1,0:T(4,128)} %basis.1, s32[1,32]{1,0:T(1,128)} %bitcast.13, ...), custom_call_target="tpu_custom_call" | custom-call | flops 8000000000 | bytes 12000000 | tf_op jit(solution)/shard_map/interaction_grads/pallas_call | solution.py:637
  77.5 2.1 %clip.1 = (f32[2,4,4,512]{3,2,1,0:T(4,128)}, f32[2,8,64]{2,1,0:T(8,128)}, f32[2,16,64]{2,1,0:T(8,128)}, f32[2,4,4,512]{3,2,1,0:T(4,128)}, f32[2,4,89]{2,1,0:T(4,128)}, /*index=5*/bf16[512,512]{1,0:T(8,128)(2,1)}) custom-call(f32[8,8,512]{2,1,0:T(8,128)} %get-tuple-element.17.fin, f32[16,128]{1,0:T(8,128)} %get-tuple-element.18.fin_s, ...), custom_call_target="tpu_custom_call" | custom-call | tf_op jit(solution)/shard_map/clip/pallas_call | solution.py:655

commit v4 on v3

--- a/solution.py
+++ b/solution.py
@@ -109,13 +109,13 @@
 
 def kernel(
     counts, send, ang, basis, spec, w_first, feat_h, cot_h, gain_h, wup_h, wsec_h, wout_h,
-    fin, fin_s, fin_g, sums, fg_o,
+    fin_h, fin_sh, fin_gh, sums, fg_o,
     feat, cot, gain, wup, wout, wsec, wfp, gpad, wsem,
     xb, lg, rad, pre, hid, sm, mx, grow, abc, lbuf, dyb, dmx, dsb, dr, dl, turn, xt, pt, dsk, fgb,
     own, own_s, own_g, outb, outb_s, outb_g,
     rx0, rx0_s, rx0_g, rx1, rx1_s, rx1_g, rx2, rx2_s, rx2_g,
     f2, f2_s, f2_g, s3, s3_s, s3_g, rx3, rx3_s, rx3_g,
-    red, redrx,
+    fin, fin_s, fin_g, red, redrx,
     ss0, rs0, ss1, rs1, ss2, rs2, ss3, rs3, ssr, rsr,
 ):
     x, c, z, y = position()
@@ -550,6 +550,9 @@
             one.start()
         redrx[base + p] = red[stage]
         if stage == 0:
+            for q, (src, dst) in enumerate(((fin, fin_h), (fin_s, fin_sh), (fin_g, fin_gh))):
+                saves.append(pltpu.make_async_copy(src, dst, wsem.at[10 + q]))
+                saves[-1].start()
             for u in range(NUNITS):
                 if not (u < 16 and u + OUT_SLOTS < 16):
                     step0(u).wait_send()
@@ -569,7 +572,8 @@
     for stage, n in GROUPS:
         for copy in all_sum(stage, n)[0]:
             copy.wait_send()
-    saves[0].wait()
+    for one in saves:
+        one.wait()
 
 
 def finish(fin, fin_s, fin_g, sums, fg, up_o, first_o, sec_o, out_o, gain_o, fg_o):
@@ -599,7 +603,7 @@
     dma = pltpu.SemaphoreType.DMA
     scratch = [
         V((C, C), BF16), V((C, C), BF16), V((89, 2, C), F32),
-        V((2, 4, C, C), BF16), V((2, 4, C, C), BF16), V((2, 128, 2048), BF16), V((2, 8, 128), F32), V((2, 128, C), F32), dma((10,)),
+        V((2, 4, C, C), BF16), V((2, 4, C, C), BF16), V((2, 128, 2048), BF16), V((2, 8, 128), F32), V((2, 128, C), F32), dma((13,)),
         V((2, C, C), BF16),
         V((2, 16, EDGES, C), BF16),
         V((2, EDGES, 2048), F32),
@@ -628,6 +632,7 @@
         V((16, 16, C), F32), V((64, 128), F32), V((16, 256), F32),
         V((NPAIRS, 4, 8, C), F32), V((4, 16, 128), F32), V((4, 8, 128), F32),
         V((NPAIRS, 3, 8, C), F32), V((3, 16, 128), F32), V((3, 8, 128), F32),
+        V((NPAIRS, 8, C), F32), V((16, 128), F32), V((8, 128), F32),
         V((3, 16, 128), F32), V((24, 16, 128), F32),
         dma((NUNITS,)), dma((NUNITS,)), dma((6 * NUNITS,)), dma((6 * NUNITS,)),
         dma((3 * NUNITS,)), dma((3 * NUNITS,)), dma((3 * (NPAIRS + 2),)), dma((3 * (NPAIRS + 2),)),
@@ -642,7 +647,7 @@
             shape((C, C), BF16),
         ),
         in_specs=[pl.BlockSpec(memory_space=pltpu.SMEM)] + [vm] * 5 + [hbm] * 6,
-        out_specs=(vm,) * 4 + (hbm,),
+        out_specs=(hbm,) * 3 + (vm, hbm),
         scratch_shapes=scratch,
         compiler_params=pltpu.CompilerParams(
             collective_id=0, has_side_effects=True, vmem_limit_bytes=63 * 2**20

time: 79.8 us -> 79.8 us (level)
  no operation moved by 1% of the time
where the time goes in v4:
time: 79.8 us; the launch traced here: 79.5 us
  Pallas kernels  78.3 us (98%)
  between operations  1.29 us (2%)
    pallas_call x1, Pallas kernels, per_device(): pl.pallas_call(kernel, name='interaction_grads', out_shape=(shape((NPAIRS...  76.1 us
    pallas_call x1, Pallas kernels, per_device(): pl.pallas_call(finish, name='clip', out_shape=(shape((2, 4, 4, C), F32),...  2.1 us

profile of v4, /device:TPU:1, one launch (start us, length us, event | category | flops | bytes accessed | tf_op | source)
XLA Modules:
  0.0 79.5 jit_solution(371091456919954214)
XLA Ops:
  1.3 76.1 %interaction_grads.1 = (f32[8,8,512]{2,1,0:T(8,128)}, f32[16,128]{1,0:T(8,128)}, f32[8,128]{1,0:T(8,128)}, f32[16,128]{1,0:T(8,128)}, bf16[512,512]{1,0:T(8,128)(2,1)}) custom-call(s32[1]{0:T(128)S(6)} %copy.18.counts, s32[4,32]{1,0:T(4,128)} %send.1, f32[16,4,32]{2,1,0:T(4,128)} %ang.1, f32[8,4,32]{2,1,0:T(4,128)} %basis.1, s32[1,32]{1,0:T(1,128)} %bitcast.13, ...), custom_call_target="tpu_custom_call" | custom-call | flops 8000000000 | bytes 12000000 | tf_op jit(solution)/shard_map/interaction_grads/pallas_call | solution.py:642
  77.4 2.1 %clip.1 = (f32[2,4,4,512]{3,2,1,0:T(4,128)}, f32[2,8,64]{2,1,0:T(8,128)}, f32[2,16,64]{2,1,0:T(8,128)}, f32[2,4,4,512]{3,2,1,0:T(4,128)}, f32[2,4,89]{2,1,0:T(4,128)}, /*index=5*/bf16[512,512]{1,0:T(8,128)(2,1)}) custom-call(f32[8,8,512]{2,1,0:T(8,128)} %get-tuple-element.17.fin, f32[16,128]{1,0:T(8,128)} %get-tuple-element.18.fin_s, ...), custom_call_target="tpu_custom_call" | custom-call | tf_op jit(solution)/shard_map/clip/pallas_call | solution.py:660
